TPU v7x, 128 devices: a whole 4x4x4 slice. The times are simulated.
128 devices in a mesh: seq: 16 (over x_hi, y, core), fsdp: 8 (over z, x_lo).
Axes of the slice: x: 4 (x_hi: 2, x_lo: 2; x = x_hi * 2 + x_lo), y: 4, z: 4, core: 2. Of those that a mesh axis runs over, the one named last changes fastest.
Arguments:
- tokens: bfloat16 [8, 2048, 1024], P('fsdp', 'seq'), may hold values from -6 to 6
- segment: int32 [8, 2048], P('fsdp'), may hold values from 0 to 8, as said below
- ln_gain: bfloat16 [2, 1024], P(None, 'fsdp'), may hold values from 0.5 to 2
- ln_bias: bfloat16 [2, 1024], P(None, 'fsdp'), may hold values from -3 to 3
- w_qkv: bfloat16 [2, 1024, 3072], P(None, 'fsdp'), may hold values from -0.1875 to 0.1875
- w_out: bfloat16 [2, 1024, 1024], P(None, 'fsdp'), may hold values from -0.75 to 0.75
- w_in: bfloat16 [2, 1024, 4096], P(None, 'fsdp'), may hold values from -0.1875 to 0.1875
- b_in: bfloat16 [2, 4096], P(None, 'fsdp'), may hold values from -4 to 4
- w_fc: bfloat16 [2, 4096, 1024], P(None, 'fsdp'), may hold values from -0.09375 to 0.09375
- b_fc: bfloat16 [2, 1024], P(None, 'fsdp'), may hold values from -3 to 3
- cotangent: bfloat16 [8, 2048, 1024], P('fsdp', 'seq'), may hold values from -6 to 6
Outputs:
- mixed_out: bfloat16 [8, 2048, 1024], P('fsdp', 'seq')
- grad_tokens: float32 [8, 2048, 1024], P('fsdp', 'seq')
- grad_gain: float32 [2, 1024], P(None, 'fsdp')
- grad_shift: float32 [2, 1024], P(None, 'fsdp')
- grad_qkv: float32 [2, 1024, 3072], P(None, 'fsdp')
- grad_out: float32 [2, 1024, 1024], P(None, 'fsdp')
- grad_in: float32 [2, 1024, 4096], P(None, 'fsdp')
- grad_in_bias: float32 [2, 4096], P(None, 'fsdp')
- grad_fc: float32 [2, 4096, 1024], P(None, 'fsdp')
- grad_fc_bias: float32 [2, 1024], P(None, 'fsdp')
Inputs may be any that keep to these rules, and one draw needn't show every extreme that they name: Within each group segment numbers never fall along the tokens; the prompt (segment 0) holds 1040 to 1536 tokens; every continuation holds one token or more.
All inputs are finite; a program needn't handle non-finite values.
Results may differ from a plain program's by a relative error of at most 0.022.
Values may be sent and summed in bfloat16 or wider, within the bound.
No kernel may reach another device: no remote copies, remote signals or barrier semaphores. Data moves between devices by JAX's collectives and lax.ppermute only.
A program may use at most 256 MiB of HBM per device.

v0:
```python
import jax
import jax.numpy as jnp
from jax import lax
from jax.sharding import PartitionSpec as P

HEADS = 16
ROT = 32
LAYERS = 2
CONTS = 8


def positions_of(group_seg):
    token_index = jnp.arange(group_seg.shape[0], dtype=jnp.int32)
    labels = jnp.arange(CONTS + 1, dtype=jnp.int32)
    member = (group_seg[:, None] == labels[None, :]).astype(jnp.int32)
    counts = jnp.sum(member, axis=0)
    starts = jnp.cumsum(counts) - counts
    own_start = jnp.sum(member * starts[None, :], axis=1)
    return token_index - own_start + jnp.where(group_seg > 0, counts[0], 0)


def angles(positions):
    half = ROT // 2
    inverse = 10000.0 ** (-2.0 * jnp.arange(half, dtype=jnp.float32) / ROT)
    phase = positions.astype(jnp.float32)[:, None] * inverse[None, :]
    return (jnp.cos(phase), jnp.sin(phase))


def rotate(field, cosine, sine):
    lead = field.shape[:-1]
    pairs = field[..., :ROT].reshape(lead + (ROT // 2, 2))
    even = pairs[..., 0]
    odd = pairs[..., 1]
    cos_b = cosine[:, None, :]
    sin_b = sine[:, None, :]
    turned = jnp.stack([even * cos_b - odd * sin_b, odd * cos_b + even * sin_b], axis=-1).reshape(
        lead + (ROT,)
    )
    return jnp.concatenate([turned, field[..., ROT:]], axis=-1)


def norm_part(inputs, gain, shift):
    average = jnp.mean(inputs, axis=-1, keepdims=True)
    centred = inputs - average
    variance = jnp.mean(centred * centred, axis=-1, keepdims=True)
    return centred * lax.rsqrt(variance + 1e-05) * gain + shift


def gelu_part(inputs):
    return jax.nn.gelu(inputs, approximate=True)


def visible(row_start, block_len, group_seg):
    key_index = jnp.arange(group_seg.shape[0], dtype=jnp.int32)
    row_index = row_start + jnp.arange(block_len, dtype=jnp.int32)
    row_seg = lax.dynamic_slice_in_dim(group_seg, row_start, block_len, 0)
    same = (group_seg[None, :] == 0) | (group_seg[None, :] == row_seg[:, None])
    return (key_index[None, :] <= row_index[:, None]) & same


def fetch(shards, layer_no):
    return (
        lax.all_gather(shards[0][layer_no], "fsdp", axis=0, tiled=True),
        lax.all_gather(shards[1][layer_no], "fsdp", axis=0, tiled=True),
        lax.all_gather(shards[2][layer_no], "fsdp", axis=0, tiled=True),
        lax.all_gather(shards[3][layer_no], "fsdp", axis=0, tiled=True),
        lax.all_gather(shards[4][layer_no], "fsdp", axis=0, tiled=True),
        lax.all_gather(shards[5][layer_no], "fsdp", axis=0, tiled=True),
        lax.all_gather(shards[6][layer_no], "fsdp", axis=0, tiled=True),
        lax.all_gather(shards[7][layer_no], "fsdp", axis=0, tiled=True),
    )


def reduce_all(stacked):
    owned = (
        lax.psum_scatter(
            stacked[0].astype(jnp.bfloat16), "fsdp", scatter_dimension=1, tiled=True
        ).astype(jnp.float32),
        lax.psum_scatter(
            stacked[1].astype(jnp.bfloat16), "fsdp", scatter_dimension=1, tiled=True
        ).astype(jnp.float32),
        lax.psum_scatter(
            stacked[2].astype(jnp.bfloat16), "fsdp", scatter_dimension=1, tiled=True
        ).astype(jnp.float32),
        lax.psum_scatter(
            stacked[3].astype(jnp.bfloat16), "fsdp", scatter_dimension=1, tiled=True
        ).astype(jnp.float32),
        lax.psum_scatter(
            stacked[4].astype(jnp.bfloat16), "fsdp", scatter_dimension=1, tiled=True
        ).astype(jnp.float32),
        lax.psum_scatter(
            stacked[5].astype(jnp.bfloat16), "fsdp", scatter_dimension=1, tiled=True
        ).astype(jnp.float32),
        lax.psum_scatter(
            stacked[6].astype(jnp.bfloat16), "fsdp", scatter_dimension=1, tiled=True
        ).astype(jnp.float32),
        lax.psum_scatter(
            stacked[7].astype(jnp.bfloat16), "fsdp", scatter_dimension=1, tiled=True
        ).astype(jnp.float32),
    )
    return (
        lax.psum(owned[0].astype(jnp.bfloat16), "seq").astype(jnp.float32),
        lax.psum(owned[1].astype(jnp.bfloat16), "seq").astype(jnp.float32),
        lax.psum(owned[2].astype(jnp.bfloat16), "seq").astype(jnp.float32),
        lax.psum(owned[3].astype(jnp.bfloat16), "seq").astype(jnp.float32),
        lax.psum(owned[4].astype(jnp.bfloat16), "seq").astype(jnp.float32),
        lax.psum(owned[5].astype(jnp.bfloat16), "seq").astype(jnp.float32),
        lax.psum(owned[6].astype(jnp.bfloat16), "seq").astype(jnp.float32),
        lax.psum(owned[7].astype(jnp.bfloat16), "seq").astype(jnp.float32),
    )


def attention_forward(queries, keys_rot, values, group_seg):
    length, local_heads, head_dim = queries.shape
    block_len = min(512, length)
    scaling = head_dim ** (-0.5)

    def one_block(row_start):
        rows_q = lax.dynamic_slice_in_dim(queries, row_start, block_len, 0)
        allowed = visible(row_start, block_len, group_seg)
        scores = (
            jnp.einsum("qhd,khd->hqk", rows_q, keys_rot, preferred_element_type=jnp.float32)
            * scaling
        )
        scores = jnp.where(allowed[None], scores, -1e30)
        row_max = jnp.max(scores, axis=-1, keepdims=True)
        exponent = jnp.exp(scores - row_max)
        row_sum = jnp.sum(exponent, axis=-1, keepdims=True)
        attn_probs = (exponent / row_sum).astype(jnp.bfloat16)
        mixed = jnp.einsum("hqk,khd->qhd", attn_probs, values, preferred_element_type=jnp.float32)
        return (mixed.astype(jnp.bfloat16), (row_max + jnp.log(row_sum))[..., 0])

    starts = jnp.arange(length // block_len, dtype=jnp.int32) * block_len
    mixed, log_sums = lax.map(one_block, starts)
    return (mixed.reshape(length, local_heads, head_dim), log_sums)


def attention_backward(queries, keys_rot, values, log_sums, grad_mixed, group_seg):
    length, local_heads, head_dim = queries.shape
    block_len = min(512, length)
    scaling = head_dim ** (-0.5)

    def one_block(sums, block_item):
        key_sum, value_sum = sums
        row_start, log_sum = block_item
        rows_q = lax.dynamic_slice_in_dim(queries, row_start, block_len, 0)
        rows_grad = lax.dynamic_slice_in_dim(grad_mixed, row_start, block_len, 0)
        allowed = visible(row_start, block_len, group_seg)
        scores = (
            jnp.einsum("qhd,khd->hqk", rows_q, keys_rot, preferred_element_type=jnp.float32)
            * scaling
        )
        attn_probs = jnp.where(allowed[None], jnp.exp(scores - log_sum[..., None]), 0.0)
        d_probs = jnp.einsum("qhd,khd->hqk", rows_grad, values, preferred_element_type=jnp.float32)
        inner = jnp.sum(attn_probs * d_probs, axis=-1, keepdims=True)
        d_scores = (attn_probs * (d_probs - inner)).astype(jnp.bfloat16)
        d_rows = (
            jnp.einsum("hqk,khd->qhd", d_scores, keys_rot, preferred_element_type=jnp.float32)
            * scaling
        )
        key_sum = (
            key_sum
            + jnp.einsum("hqk,qhd->khd", d_scores, rows_q, preferred_element_type=jnp.float32)
            * scaling
        )
        value_sum = value_sum + jnp.einsum(
            "hqk,qhd->khd",
            attn_probs.astype(jnp.bfloat16),
            rows_grad,
            preferred_element_type=jnp.float32,
        )
        return ((key_sum, value_sum), d_rows)

    zeros = jnp.zeros((length, local_heads, head_dim), jnp.float32)
    starts = jnp.arange(length // block_len, dtype=jnp.int32) * block_len
    (d_keys, d_values), d_blocks = lax.scan(one_block, (zeros, zeros), (starts, log_sums))
    return (d_blocks.reshape(length, local_heads, head_dim), d_keys, d_values)


def forward_layer(hidden, weights, group_seg, cosine, sine):
    gain, shift, w_q, w_o, w_i, bias_i, w_f, bias_f = weights
    tok_rows, width = hidden.shape
    head_dim = width // HEADS
    normed = norm_part(hidden, gain.astype(jnp.float32), shift.astype(jnp.float32)).astype(
        jnp.bfloat16
    )
    joined = jnp.dot(normed, w_q, preferred_element_type=jnp.float32).astype(jnp.bfloat16)
    joined = joined.reshape(tok_rows, 3, HEADS, head_dim)
    spread = lax.all_to_all(joined, "seq", split_axis=2, concat_axis=0, tiled=True)
    queries = rotate(spread[:, 0].astype(jnp.float32), cosine, sine).astype(jnp.bfloat16)
    keys_rot = rotate(spread[:, 1].astype(jnp.float32), cosine, sine).astype(jnp.bfloat16)
    values = spread[:, 2]
    mixed, log_sums = attention_forward(queries, keys_rot, values, group_seg)
    gathered = lax.all_to_all(mixed, "seq", split_axis=0, concat_axis=1, tiled=True).reshape(
        tok_rows, width
    )
    branch = jnp.dot(gathered, w_o, preferred_element_type=jnp.float32)
    pre_act = jnp.dot(normed, w_i, preferred_element_type=jnp.float32) + bias_i.astype(jnp.float32)
    active = gelu_part(pre_act).astype(jnp.bfloat16)
    feed = jnp.dot(active, w_f, preferred_element_type=jnp.float32) + bias_f.astype(jnp.float32)
    saved = (hidden, normed, queries, keys_rot, values, log_sums, gathered, pre_act, active)
    return (hidden + branch + feed, saved)


def backward_layer(upstream, weights, saved, group_seg, cosine, sine):
    gain, shift, w_q, w_o, w_i, bias_i, w_f, bias_f = weights
    hidden, normed, queries, keys_rot, values, log_sums, gathered, pre_act, active = saved
    tok_rows, width = hidden.shape
    head_dim = width // HEADS
    grad_low = upstream.astype(jnp.bfloat16)
    d_bias_f = jnp.sum(upstream, axis=0)
    d_w_f = jnp.einsum("tf,td->fd", active, grad_low, preferred_element_type=jnp.float32)
    d_active = jnp.einsum("td,fd->tf", grad_low, w_f, preferred_element_type=jnp.float32)
    unused, gelu_pull = jax.vjp(gelu_part, pre_act)
    d_pre = gelu_pull(d_active)[0]
    d_bias_i = jnp.sum(d_pre, axis=0)
    d_pre_low = d_pre.astype(jnp.bfloat16)
    d_w_i = jnp.einsum("td,tf->df", normed, d_pre_low, preferred_element_type=jnp.float32)
    d_normed = jnp.einsum("tf,df->td", d_pre_low, w_i, preferred_element_type=jnp.float32)
    d_w_o = jnp.einsum("tc,td->cd", gathered, grad_low, preferred_element_type=jnp.float32)
    d_mixed = jnp.einsum("td,cd->tc", grad_low, w_o, preferred_element_type=jnp.float32).astype(
        jnp.bfloat16
    )
    d_heads = lax.all_to_all(
        d_mixed.reshape(tok_rows, HEADS, head_dim), "seq", split_axis=1, concat_axis=0, tiled=True
    )
    d_queries, d_keys, d_values = attention_backward(
        queries, keys_rot, values, log_sums, d_heads, group_seg
    )
    stacked = jnp.stack(
        [rotate(d_queries, cosine, -sine), rotate(d_keys, cosine, -sine), d_values], axis=1
    )
    d_joined = lax.all_to_all(
        stacked.astype(jnp.bfloat16), "seq", split_axis=0, concat_axis=2, tiled=True
    )
    d_joined = d_joined.reshape(tok_rows, 3 * width)
    d_w_q = jnp.einsum("td,tc->dc", normed, d_joined, preferred_element_type=jnp.float32)
    d_normed = d_normed + jnp.einsum("tc,dc->td", d_joined, w_q, preferred_element_type=jnp.float32)
    unused_out, norm_pull = jax.vjp(
        norm_part, hidden, gain.astype(jnp.float32), shift.astype(jnp.float32)
    )
    d_hidden, d_gain, d_shift = norm_pull(d_normed)
    grads = (d_gain, d_shift, d_w_q, d_w_o, d_w_i, d_bias_i, d_w_f, d_bias_f)
    return (upstream + d_hidden, grads)


def body(tokens, segment, ln_gain, ln_bias, w_qkv, w_out, w_in, b_in, w_fc, b_fc, cotangent):
    shards = (ln_gain, ln_bias, w_qkv, w_out, w_in, b_in, w_fc, b_fc)
    group_seg = segment[0]
    cosine, sine = angles(positions_of(group_seg))
    hidden = tokens[0].astype(jnp.float32)
    kept_weights = []
    saved_all = []
    for layer_no in range(LAYERS):
        weights = fetch(shards, layer_no)
        hidden, saved = forward_layer(hidden, weights, group_seg, cosine, sine)
        kept_weights.append(weights)
        saved_all.append(saved)
    upstream = cotangent[0].astype(jnp.float32)
    layer_grads = [None] * LAYERS
    for layer_no in reversed(range(LAYERS)):
        weights = kept_weights[layer_no]
        upstream, grads = backward_layer(
            upstream, weights, saved_all[layer_no], group_seg, cosine, sine
        )
        layer_grads[layer_no] = grads
    stacked = tuple(
        (
            jnp.stack([layer_grads[layer_no][member] for layer_no in range(LAYERS)])
            for member in range(8)
        )
    )
    outputs = reduce_all(stacked)
    return (
        hidden.astype(jnp.bfloat16)[None],
        upstream[None],
        outputs[0],
        outputs[1],
        outputs[2],
        outputs[3],
        outputs[4],
        outputs[5],
        outputs[6],
        outputs[7],
    )


def solution(mesh):
    in_specs = (
        P("fsdp", "seq", None),
        P("fsdp", None),
        P(None, "fsdp"),
        P(None, "fsdp"),
        P(None, "fsdp", None),
        P(None, "fsdp", None),
        P(None, "fsdp", None),
        P(None, "fsdp"),
        P(None, "fsdp", None),
        P(None, "fsdp"),
        P("fsdp", "seq", None),
    )
    out_specs = (
        P("fsdp", "seq", None),
        P("fsdp", "seq", None),
        P(None, "fsdp"),
        P(None, "fsdp"),
        P(None, "fsdp", None),
        P(None, "fsdp", None),
        P(None, "fsdp", None),
        P(None, "fsdp"),
        P(None, "fsdp", None),
        P(None, "fsdp"),
    )
    return jax.shard_map(body, mesh=mesh, in_specs=in_specs, out_specs=out_specs, check_vma=False)
```

profile of v0, /device:TPU:1, one launch (start us, length us, event | category | flops | bytes accessed | tf_op | source)
XLA Modules:
  0.0 2494.7 jit_solution(10763223247228091560)
XLA Ops:
  20.2 17.7 all-gather.7
  91.3 21.0 all-gather.13
  112.3 21.0 all-gather.5
  148.9 18.3 all-to-all-start
  167.3 22.6 all-to-all-done
  192.1 27.7 %while.54 = (s32[]{:T(128)}, bf16[4,512,1,64]{1,3,2,0:T(8,128)(2,1)S(1)}, f32[4,1,512]{2,1,0:T(1,128)S(1)}, s32[4]{0:T(128)S(1)}, s32[1,2048]{1,0:T(1,128)S(1)},...) while((s32[]{:T(128)}, ...), condition=%wide.region_8.9_spmd, body=%wide.region_5.8_spmd.sunk | while | flops 281053184 | bytes 13289663 | solution.py:134
  262.6 119.6 %all-gather.29.cloned.1.call-done = bf16[1,1024,4096]{2,1,0:T(8,128)(2,1)} async-done(((bf16[1,128,4096]{2,1,0:T(8,128)(2,1)}), bf16[1,1024,4096]{2,1,0:T(8,128)(2,1)}) %all-gather.29.cloned.1.call-update) | async-done | bytes 8388624 | tf_op jit(solution)/shard_map/all_gather | solution.py:67
  388.2 165.4 %all-gather.31.cloned.1.call-done = bf16[1,4096,1024]{2,1,0:T(8,128)(2,1)} async-done(((bf16[1,512,1024]{2,1,0:T(8,128)(2,1)}), bf16[1,4096,1024]{2,1,0:T(8,128)(2,1)}) %all-gather.31.cloned.1.call-update) | async-done | bytes 8388624 | tf_op jit(solution)/shard_map/all_gather | solution.py:69
  559.3 49.1 %all-gather.27.cloned.1.call-done = bf16[1,1024,1024]{2,1,0:T(8,128)(2,1)} async-done(((bf16[1,128,1024]{2,1,0:T(8,128)(2,1)}), bf16[1,1024,1024]{2,1,0:T(8,128)(2,1)}) %all-gather.27.cloned.1.call-update) | async-done | bytes 2097168 | tf_op jit(solution)/shard_map/all_gather | solution.py:66
  610.9 128.2 %all-gather.33.cloned.1.call-done = bf16[1,1024,3072]{2,1,0:T(8,128)(2,1)} async-done(((bf16[1,128,3072]{2,1,0:T(8,128)(2,1)}), bf16[1,1024,3072]{2,1,0:T(8,128)(2,1)}) %all-gather.33.cloned.1.call-update) | async-done | bytes 6291472 | tf_op jit(solution)/shard_map/all_gather | solution.py:65
  752.6 166.3 %all-gather.37.cloned.1.call-done = bf16[1,1024,4096]{2,1,0:T(8,128)(2,1)} async-done(((bf16[1,128,4096]{2,1,0:T(8,128)(2,1)}), bf16[1,1024,4096]{2,1,0:T(8,128)(2,1)}) %all-gather.37.cloned.1.call-update) | async-done | bytes 8388624 | tf_op jit(solution)/shard_map/all_gather | solution.py:67
  927.0 27.7 %while.55 = (s32[]{:T(128)}, bf16[4,512,1,64]{1,3,2,0:T(8,128)(2,1)S(1)}, f32[4,1,512]{2,1,0:T(1,128)S(1)}, s32[4]{0:T(128)S(1)}, s32[1,2048]{1,0:T(1,128)S(1)},...) while((s32[]{:T(128)}, ...), condition=%wide.region_14.15_spmd, body=%wide.region_11.14_spmd.sunk | while | flops 281053184 | bytes 13289663 | solution.py:134
  955.4 41.8 %while.56 = (s32[]{:T(128)}, f32[2048,1,64]{0,2,1:T(8,128)S(1)}, f32[2048,1,64]{0,2,1:T(8,128)S(1)}, f32[4,512,1,64]{1,0,3,2:T(4,128)S(1)}, s32[4]{0:T(128)S(1)}...) while((s32[]{:T(128)}, f32[2048,1,64]{0,2,1:T(8,128)S(1)}, ...), condition=%wide.region_17.18_spmd.clone, body=%wide.region_15.17_spmd.clone.sunk | while | flops 685410304 | bytes 35299564 | solution.py:176
  1037.1 64.1 %all-gather.39.cloned.1.call-done = bf16[1,4096,1024]{2,1,0:T(8,128)(2,1)} async-done(((bf16[1,512,1024]{2,1,0:T(8,128)(2,1)}), bf16[1,4096,1024]{2,1,0:T(8,128)(2,1)}) %all-gather.39.cloned.1.call-update) | async-done | bytes 8388624 | tf_op jit(solution)/shard_map/all_gather | solution.py:69
  1153.8 42.0 %while.57 = (s32[]{:T(128)}, f32[2048,1,64]{0,2,1:T(8,128)S(1)}, f32[2048,1,64]{0,2,1:T(8,128)S(1)}, f32[4,512,1,64]{1,0,3,2:T(4,128)S(1)}, s32[4]{0:T(128)S(1)}...) while((s32[]{:T(128)}, f32[2048,1,64]{0,2,1:T(8,128)S(1)}, ...), condition=%wide.region_22.23_spmd.clone, body=%wide.region_20.22_spmd.clone.sunk | while | flops 685410304 | bytes 35299564 | solution.py:176
  1211.9 19.0 all-to-all-done.7
  1297.2 203.3 %reduce-scatter.17.cloned.1.call-done = bf16[2,128,3072]{2,1,0:T(8,128)(2,1)} async-done(((bf16[2,1024,3072]{2,1,0:T(8,128)(2,1)}), bf16[2,128,3072]{2,1,0:T(8,128)(2,1)}) %reduce-scatter.17.cloned.1.call-update) | async-done | bytes 1572880 | tf_op jit(solution)/shard_map/reduce_scatter | solution.py:82
  1500.5 330.0 %reduce-scatter.23.cloned.1.call-done = bf16[2,512,1024]{2,1,0:T(8,128)(2,1)} async-done(((bf16[2,4096,1024]{2,1,0:T(8,128)(2,1)}), bf16[2,512,1024]{2,1,0:T(8,128)(2,1)}) %reduce-scatter.23.cloned.1.call-update) | async-done | bytes 2097168 | tf_op jit(solution)/shard_map/reduce_scatter | solution.py:94
  1830.5 329.8 %reduce-scatter.21.cloned.1.call-done = bf16[2,128,4096]{2,1,0:T(8,128)(2,1)} async-done(((bf16[2,1024,4096]{2,1,0:T(8,128)(2,1)}), bf16[2,128,4096]{2,1,0:T(8,128)(2,1)}) %reduce-scatter.21.cloned.1.call-update) | async-done | bytes 2097168 | tf_op jit(solution)/shard_map/reduce_scatter | solution.py:88
  2197.1 41.9 %reduce-scatter.29.cloned.1.call-done = bf16[512,2]{1,0:T(8,128)(2,1)} async-done(((bf16[4096,2]{1,0:T(8,128)(2,1)}), bf16[512,2]{1,0:T(8,128)(2,1)}) %reduce-scatter.29.cloned.1.call-update) | async-done | bytes 2064
  2241.1 36.3 %reduce-scatter.25.cloned.1.call-done = bf16[128,2]{1,0:T(8,128)(2,1)} async-done(((bf16[1024,2]{1,0:T(8,128)(2,1)}), bf16[128,2]{1,0:T(8,128)(2,1)}) %reduce-scatter.25.cloned.1.call-update) | async-done | bytes 528
  2278.2 37.3 %reduce-scatter.27.cloned.1.call-done = bf16[128,2]{1,0:T(8,128)(2,1)} async-done(((bf16[1024,2]{1,0:T(8,128)(2,1)}), bf16[128,2]{1,0:T(8,128)(2,1)}) %reduce-scatter.27.cloned.1.call-update) | async-done | bytes 528
  2316.4 38.3 %all-reduce = (bf16[2,128]{1,0:T(2,128)(2,1)S(1)}, bf16[2,128]{1,0:T(2,128)(2,1)S(1)}, bf16[2,512]{1,0:T(2,128)(2,1)S(1)}, bf16[2,128]{1,0:T(2,128)(2,1)S(1)}) all-reduce(bf16[2,128]{1,0:T(2,128)(2,1)S(1)} %copy.274, bf16[2,128]{1,0:T(2,128)(2,1)S(1)} %copy.276, ...), channel_id=1, replica_groups=mesh['seq'=16,'fsdp'=8] {'seq'}, use_global_device_ids=true, to_apply=%region_28.29 | all-reduce | flops 1792 | bytes 7168 | tf_op jit(solution)/shard_map/psum | solution.py:102
  2357.0 121.4 %all-reduce.4.cloned.1.call-done = (bf16[2,128,3072]{2,1,0:T(8,128)(2,1)}, bf16[2,128,1024]{2,1,0:T(8,128)(2,1)}, bf16[2,128,4096]{2,1,0:T(8,128)(2,1)}, bf16[2,512,1024]{2,1,0:T(8,128)(2,1)}) async-done(((bf16[2,128,3072]{2,1,0:T(8,128)(2,1)}, bf16[2,128,1024]{2,1,0:T(8,128)(2,1)}, bf16[2,128,4096]{2,1,0:T(8,128)(2,1)}, bf16[2,512,1024]{2,1,0:T(8,128)(2,1)}), (bf16[2,128,3072]{2,1,0:T(8,128)(2,1)}, ...) | async-done | bytes 6291472 | tf_op jit(solution)/shard_map/psum | solution.py:104
  (564 shorter events, 495.4 us)
Async XLA Ops:
  7.2 136.4 %all-gather.25.cloned.1.call-start = ((), (), s32[]{:S(2)}) async-start(), calls=%async_computation.20 | async-start | bytes 7077888 | tf_op jit(solution)/shard_map/all_gather | solution.py:65
  10.0 234.5 %all-gather.35.cloned.1.call-start = ((), (), s32[]{:S(2)}) async-start(), calls=%async_computation.25 | async-start | bytes 2359296 | tf_op jit(solution)/shard_map/all_gather | solution.py:66
  11.0 371.1 %all-gather.29.cloned.1.call-start = ((), (), s32[]{:S(2)}) async-start(), calls=%async_computation.22 | async-start | bytes 9437184 | tf_op jit(solution)/shard_map/all_gather | solution.py:67
  12.6 541.1 %all-gather.31.cloned.1.call-start = ((), (), s32[]{:S(2)}) async-start(), calls=%async_computation.23 | async-start | bytes 9437184 | tf_op jit(solution)/shard_map/all_gather | solution.py:69
  15.7 592.7 %all-gather.27.cloned.1.call-start = ((), (), s32[]{:S(2)}) async-start(), calls=%async_computation.21 | async-start | bytes 2359296 | tf_op jit(solution)/shard_map/all_gather | solution.py:66
  16.3 722.9 %all-gather.33.cloned.1.call-start = ((), (), s32[]{:S(2)}) async-start(), calls=%async_computation.24 | async-start | bytes 7077888 | tf_op jit(solution)/shard_map/all_gather | solution.py:65
  16.9 902.0 %all-gather.37.cloned.1.call-start = ((), (), s32[]{:S(2)}) async-start(), calls=%async_computation.26 | async-start | bytes 9437184 | tf_op jit(solution)/shard_map/all_gather | solution.py:67
  17.6 1083.6 %all-gather.39.cloned.1.call-start = ((), (), s32[]{:S(2)}) async-start(), calls=%async_computation.27 | async-start | bytes 9437184 | tf_op jit(solution)/shard_map/all_gather | solution.py:69
  148.9 41.1 %all-to-all-start = ((bf16[128,3,16,64]{0,3,1,2:T(8,128)(2,1)}), bf16[128,3,16,64]{0,3,1,2:T(8,128)(2,1)S(1)}, u32[]{:S(2)}, u32[]{:S(2)}) async-start(bf16[128,3,16,64]{0,3,1,2:T(8,128)(2,1)} %copy.218), calls=%async_computation | async-start | bytes 1572864 | tf_op jit(solution)/shard_map/all_to_all | solution.py:189
  239.8 16.2 all-to-all-start.1
  256.1 488.2 %all-to-all-start.4 = ((bf16[128,16,64]{0,2,1:T(8,128)(2,1)}), bf16[128,16,64]{0,2,1:T(8,128)(2,1)}, u32[]{:S(2)}, u32[]{:S(2)}) async-start(bf16[128,16,64]{0,2,1:T(8,128)(2,1)} %bitcast.59), calls=%async_computation.4 | async-start | bytes 524288 | tf_op jit(solution)/shard_map/all_to_all | solution.py:224
  744.3 180.6 %all-to-all-start.2 = ((bf16[128,3,16,64]{0,3,1,2:T(8,128)(2,1)}), bf16[128,3,16,64]{0,3,1,2:T(8,128)(2,1)S(1)}, u32[]{:S(2)}, u32[]{:S(2)}) async-start(bf16[128,3,16,64]{0,3,1,2:T(8,128)(2,1)} %copy.231), calls=%async_computation.2 | async-start | bytes 1572864 | tf_op jit(solution)/shard_map/all_to_all | solution.py:189
  1012.7 18.8 all-to-all-start.3
  1031.5 81.3 %all-to-all-start.5 = ((bf16[16,2,12288]{2,1,0:T(2,128)(2,1)}), bf16[16,2,12288]{2,1,0:T(2,128)(2,1)}, u32[]{:S(2)}, u32[]{:S(2)}) async-start(bf16[16,2,12288]{2,1,0:T(2,128)(2,1)} %reshape.1332), calls=%async_computation.5 | async-start | bytes 1572864 | tf_op jit(solution)/shard_map/all_to_all | solution.py:233
  1145.0 152.2 %reduce-scatter.19.cloned.1.call-start = ((), (), s32[]{:S(2)}) async-start(), calls=%async_computation.17 | async-start | bytes 4718592 | tf_op jit(solution)/shard_map/reduce_scatter | solution.py:85
  1202.2 28.7 %all-to-all-start.7 = ((bf16[16,2,12288]{2,1,0:T(2,128)(2,1)}), bf16[16,2,12288]{2,1,0:T(2,128)(2,1)}, u32[]{:S(2)}, u32[]{:S(2)}) async-start(bf16[16,2,12288]{2,1,0:T(2,128)(2,1)} %reshape.1334), calls=%async_computation.7 | async-start | bytes 1572864 | tf_op jit(solution)/shard_map/all_to_all | solution.py:233
  1207.3 293.2 %reduce-scatter.17.cloned.1.call-start = ((), (), s32[]{:S(2)}) async-start(), calls=%async_computation.16 | async-start | bytes 14155776 | tf_op jit(solution)/shard_map/reduce_scatter | solution.py:82
  1245.1 585.5 %reduce-scatter.23.cloned.1.call-start = ((), (), s32[]{:S(2)}) async-start(), calls=%async_computation.19 | async-start | bytes 18874368 | tf_op jit(solution)/shard_map/reduce_scatter | solution.py:94
  1259.3 901.1 %reduce-scatter.21.cloned.1.call-start = ((), (), s32[]{:S(2)}) async-start(), calls=%async_computation.18 | async-start | bytes 18874368 | tf_op jit(solution)/shard_map/reduce_scatter | solution.py:88
  1279.5 916.7 %reduce-scatter.31.cloned.1.call-start = ((), (), s32[]{:S(2)}) async-start(), calls=%async_computation.31 | async-start | bytes 294912
  1280.7 958.3 %reduce-scatter.29.cloned.1.call-start = ((), (), s32[]{:S(2)}) async-start(), calls=%async_computation.30 | async-start | bytes 1179648
  1282.2 995.2 %reduce-scatter.25.cloned.1.call-start = ((), (), s32[]{:S(2)}) async-start(), calls=%async_computation.28 | async-start | bytes 294912
  1296.2 1019.4 %reduce-scatter.27.cloned.1.call-start = ((), (), s32[]{:S(2)}) async-start(), calls=%async_computation.29 | async-start | bytes 294912
  1297.1 1181.3 %all-reduce.4.cloned.1.call-start = ((), (), s32[]{:S(2)}) async-start(), calls=%async_computation.32 | async-start | bytes 12582912 | tf_op jit(solution)/shard_map/psum | solution.py:104
  (61 other events, 2580.4 us)
Sparse Core Ops, SparseCore 0:
  10.2 133.4 all-gather.24
  145.3 61.3 all-gather.34
  208.9 173.2 all-gather.28
  384.2 169.3 all-gather.30
  555.2 53.1 all-gather.26
  610.5 128.6 all-gather.32
  741.4 177.4 all-gather.36
  920.5 180.6 all-gather.38
  1149.2 100.8 reduce-scatter.18
  1252.4 248.1 reduce-scatter.16
  1503.0 327.4 reduce-scatter.22
  1832.9 327.4 reduce-scatter.20
  2162.7 33.5 reduce-scatter.30
  2199.2 39.7 reduce-scatter.28
  2241.3 36.0 reduce-scatter.24
  2279.6 35.9 reduce-scatter.26
  2318.4 159.9 all-reduce.3
where the time goes:
time: 2500 us; the launch traced here: 2490 us
  waiting for transfers between devices  1880 us (75%)
  blocking collectives  165 us (7%)
  matrix products  164 us (7%)
  local copies, waits for them, and re-layouts  92.8 us (4%)
  other arithmetic  82.9 us (3%)
  starting transfers between devices  61.6 us (2%)
  loops' own time  32.6 us (1%)
    reduce_scatter x1, waiting for transfers between devices, reduce_all(): lax.psum_scatter(stacked[6].astype(jnp.bfloat16), 'fsdp', scatter_dimensi...  330 us
    reduce_scatter x1, waiting for transfers between devices, reduce_all(): lax.psum_scatter(stacked[4].astype(jnp.bfloat16), 'fsdp', scatter_dimensi...  330 us
    all_gather x2, waiting for transfers between devices, fetch(): lax.all_gather(shards[4][layer_no], 'fsdp', axis=0, tiled=True)  286 us
    all_gather x2, waiting for transfers between devices, fetch(): lax.all_gather(shards[6][layer_no], 'fsdp', axis=0, tiled=True)  230 us
    reduce_scatter x1, waiting for transfers between devices, reduce_all(): lax.psum_scatter(stacked[2].astype(jnp.bfloat16), 'fsdp', scatter_dimensi...  203 us
    all_gather x2, waiting for transfers between devices, fetch(): lax.all_gather(shards[2][layer_no], 'fsdp', axis=0, tiled=True)  139 us
    unnamed x21, waiting for transfers between devices  134 us
    psum x1, waiting for transfers between devices, reduce_all(): lax.psum(owned[2].astype(jnp.bfloat16), 'seq').astype(jnp.float32)  121 us
  transfers between devices with their start and end apart: 25, of which 20 were waited for; matrix products, arithmetic and copies ran while one was open for 12% of the time, Pallas kernels for 0%

commit v1 on v0

v1 whole, which is shorter than its diff:
```python
import functools
import numpy as np
import jax
import jax.numpy as jnp
from jax import lax
from jax.experimental import pallas as pl
from jax.experimental.pallas import tpu as pltpu
from jax.sharding import Mesh, PartitionSpec as P

HEADS = 16
ROT = 32
LAYERS = 2
CONTS = 8
D = 1024
FF = 4096
HALF = 1024
BLK = 128
QB = 256
AXES = ("xh", "y", "core", "z", "xl")
FS = ("z", "xl")
f32 = jnp.float32
bf16 = jnp.bfloat16
NT = (((1,), (1,)), ((), ()))


def shift(x, axis, by, size):
    return lax.ppermute(x, axis, [(i, (i + by) % size) for i in range(size)])


def pick(x, index, axis=0):
    return lax.dynamic_index_in_dim(x, index, axis, keepdims=False)


def gather_tokens(own):
    y = lax.axis_index("y")
    c = lax.axis_index("core")
    parts = [own, shift(own, "y", -1, 4), shift(own, "y", 2, 4), shift(own, "y", 1, 4)]
    mine = jnp.stack(parts)
    other = shift(mine, "core", 1, 2)
    pair = jnp.where(c == 0, jnp.stack([mine, other], 1), jnp.stack([other, mine], 1))
    twice = jnp.concatenate([pair, pair], 0)
    ordered = lax.dynamic_slice_in_dim(twice, (4 - y) % 4, 4, 0)
    return ordered.reshape(HALF, own.shape[1])


def scatter_tokens(partial):
    y = lax.axis_index("y")
    c = lax.axis_index("core")
    blocks = partial.reshape(4, 2, BLK, partial.shape[1])
    away = pick(blocks, 1 - c, 1).astype(bf16)
    got = shift(away, "core", 1, 2)
    both = pick(blocks, c, 1).astype(f32) + got.astype(f32)
    low = both.astype(bf16)
    total = pick(both, y)
    for by in (2, 1, 3):
        total = total + shift(pick(low, (y + by) % 4), "y", by, 4).astype(f32)
    return total


def head_masks(shape, axis):
    lane = lax.broadcasted_iota(jnp.int32, shape, axis)
    return [lane < 64, lane >= 64]


def seen(i, kk, qseg_ref, kseg_ref):
    q0 = i * QB
    qs = qseg_ref[0:1, q0 : q0 + QB]
    ks = kseg_ref[0:kk, 0:1]
    key = lax.broadcasted_iota(jnp.int32, (kk, QB), 0)
    query = q0 + lax.broadcasted_iota(jnp.int32, (kk, QB), 1)
    return (key <= query) & ((ks == 0) | (ks == qs))


def attn_own_kernel(q_ref, k_ref, vt_ref, qseg_ref, kseg_ref, acc_ref, m_ref, l_ref):
    masks = head_masks((HALF, BLK), 1)
    zero = jnp.zeros((), bf16)
    km = [jnp.where(masks[h], k_ref[...], zero) for h in range(2)]
    for i in range(HALF // QB):
        cols = slice(i * QB, (i + 1) * QB)
        kk = (i + 1) * QB
        allowed = seen(i, kk, qseg_ref, kseg_ref)
        for h in range(2):
            s = lax.dot_general(km[h][:kk], q_ref[cols, :], NT, preferred_element_type=f32)
            s = jnp.where(allowed, s, -1e30)
            m = jnp.max(s, axis=0, keepdims=True)
            p = jnp.exp(s - m)
            l_ref[h : h + 1, cols] = jnp.sum(p, axis=0, keepdims=True)
            m_ref[h : h + 1, cols] = m
            rows = slice(h * 64, h * 64 + 64)
            acc_ref[rows, cols] = jnp.dot(
                vt_ref[rows, :kk], p.astype(bf16), preferred_element_type=f32
            )


def attn_full_kernel(flag_ref, q_ref, k_ref, vt_ref, acc_ref, m_ref, l_ref, out_ref, lse_ref, tmp_ref):
    upper = flag_ref[0] == 1

    @pl.when(upper)
    def _():
        masks = head_masks((HALF, BLK), 1)
        zero = jnp.zeros((), bf16)
        km = [jnp.where(masks[h], k_ref[...], zero) for h in range(2)]
        for i in range(HALF // QB):
            cols = slice(i * QB, (i + 1) * QB)
            for h in range(2):
                rows = slice(h * 64, h * 64 + 64)
                s = lax.dot_general(km[h], q_ref[cols, :], NT, preferred_element_type=f32)
                m0 = m_ref[h : h + 1, cols]
                m = jnp.maximum(m0, jnp.max(s, axis=0, keepdims=True))
                p = jnp.exp(s - m)
                a = jnp.exp(m0 - m)
                l = l_ref[h : h + 1, cols] * a + jnp.sum(p, axis=0, keepdims=True)
                o = jnp.dot(vt_ref[rows, :], p.astype(bf16), preferred_element_type=f32)
                tmp_ref[rows, cols] = (acc_ref[rows, cols] * a + o) / l
                lse_ref[h : h + 1, cols] = m + jnp.log(l)

    @pl.when(jnp.logical_not(upper))
    def _():
        for h in range(2):
            rows = slice(h * 64, h * 64 + 64)
            l = l_ref[h : h + 1, :]
            tmp_ref[rows, :] = acc_ref[rows, :] / l
            lse_ref[h : h + 1, :] = m_ref[h : h + 1, :] + jnp.log(l)

    out_ref[...] = jnp.transpose(tmp_ref[...]).astype(bf16)


def row_delta(attn_ref, do_ref):
    prod = attn_ref[...].astype(f32) * do_ref[...].astype(f32)
    head = lax.broadcasted_iota(jnp.int32, (8, BLK), 0)
    lane = lax.broadcasted_iota(jnp.int32, (8, BLK), 1) // 64
    pickers = jnp.where(head == lane, 1.0, 0.0).astype(f32)
    return lax.dot_general(
        pickers, prod, NT, precision=lax.Precision.HIGHEST, preferred_element_type=f32
    )


def grad_block(km, vm, kt, qm, dom, q_blk, do_blk, lse, delta, allowed):
    s = lax.dot_general(km, q_blk, NT, preferred_element_type=f32)
    p = jnp.exp(s - lse)
    if allowed is not None:
        p = jnp.where(allowed, p, 0.0)
    dp = lax.dot_general(vm, do_blk, NT, preferred_element_type=f32)
    ds = (p * (dp - delta)).astype(bf16)
    dqt = jnp.dot(kt, ds, preferred_element_type=f32)
    dk = jnp.dot(ds, qm, preferred_element_type=f32)
    dv = jnp.dot(p.astype(bf16), dom, preferred_element_type=f32)
    return dqt, dk, dv


def grad_setup(q_ref, k_ref, v_ref, do_ref):
    masks = head_masks((HALF, BLK), 1)
    zero = jnp.zeros((), bf16)
    cut = lambda ref: [jnp.where(masks[h], ref[...], zero) for h in range(2)]
    return cut(q_ref), cut(k_ref), cut(v_ref), cut(do_ref)


def grad_full_kernel(flag_ref, q_ref, k_ref, kt_ref, v_ref, do_ref, attn_ref, lse_ref, dqt_ref, dk_ref, dv_ref, acck, accv):
    upper = flag_ref[0] == 1

    @pl.when(upper)
    def _():
        delta = row_delta(attn_ref, do_ref)
        qm, km, vm, dom = grad_setup(q_ref, k_ref, v_ref, do_ref)
        for i in range(HALF // QB):
            cols = slice(i * QB, (i + 1) * QB)
            for h in range(2):
                rows = slice(h * 64, h * 64 + 64)
                dqt, dk, dv = grad_block(
                    km[h], vm[h], kt_ref[rows, :], qm[h][cols], dom[h][cols],
                    q_ref[cols, :], do_ref[cols, :],
                    lse_ref[h : h + 1, cols], delta[h : h + 1, cols], None,
                )
                dqt_ref[rows, cols] = dqt
                if i == 0 and h == 0:
                    acck[...] = dk
                    accv[...] = dv
                else:
                    acck[...] += dk
                    accv[...] += dv
        dk_ref[...] = acck[...].astype(bf16)
        dv_ref[...] = accv[...].astype(bf16)

    @pl.when(jnp.logical_not(upper))
    def _():
        dqt_ref[...] = jnp.zeros_like(dqt_ref)
        dk_ref[...] = jnp.zeros_like(dk_ref)
        dv_ref[...] = jnp.zeros_like(dv_ref)


def grad_own_kernel(q_ref, k_ref, kt_ref, v_ref, do_ref, attn_ref, lse_ref, qseg_ref, kseg_ref, dqt0_ref, dq_ref, dk_ref, dv_ref, tmp):
    delta = row_delta(attn_ref, do_ref)
    qm, km, vm, dom = grad_setup(q_ref, k_ref, v_ref, do_ref)
    dk_ref[...] = jnp.zeros_like(dk_ref)
    dv_ref[...] = jnp.zeros_like(dv_ref)
    for i in range(HALF // QB):
        cols = slice(i * QB, (i + 1) * QB)
        kk = (i + 1) * QB
        allowed = seen(i, kk, qseg_ref, kseg_ref)
        for h in range(2):
            rows = slice(h * 64, h * 64 + 64)
            dqt, dk, dv = grad_block(
                km[h][:kk], vm[h][:kk], kt_ref[rows, :kk], qm[h][cols], dom[h][cols],
                q_ref[cols, :], do_ref[cols, :],
                lse_ref[h : h + 1, cols], delta[h : h + 1, cols], allowed,
            )
            tmp[rows, cols] = (dqt + dqt0_ref[rows, cols]) * 0.125
            dk_ref[:kk, :] += dk
            dv_ref[:kk, :] += dv
    dq_ref[...] = jnp.transpose(tmp[...])


PARAMS = pltpu.CompilerParams(vmem_limit_bytes=48 * 1024 * 1024)
VM = pl.BlockSpec(memory_space=pltpu.VMEM)
SM = pl.BlockSpec(memory_space=pltpu.SMEM)


def shaped(*args):
    return [jax.ShapeDtypeStruct(s, t) for s, t in args]


def attn_own(q, k, vt, qseg, kseg):
    return pl.pallas_call(
        attn_own_kernel,
        out_shape=shaped(((BLK, HALF), f32), ((2, HALF), f32), ((2, HALF), f32)),
        in_specs=[VM] * 5,
        out_specs=[VM] * 3,
        compiler_params=PARAMS,
        name="attn_own",
    )(q, k, vt, qseg, kseg)


def attn_full(flag, q, k, vt, acc, m, l):
    return pl.pallas_call(
        attn_full_kernel,
        out_shape=shaped(((HALF, BLK), bf16), ((2, HALF), f32)),
        in_specs=[SM] + [VM] * 6,
        out_specs=[VM] * 2,
        scratch_shapes=[pltpu.VMEM((BLK, HALF), f32)],
        compiler_params=PARAMS,
        name="attn_full",
    )(flag, q, k, vt, acc, m, l)


def grad_full(flag, q, k, kt, v, do, attn, lse):
    return pl.pallas_call(
        grad_full_kernel,
        out_shape=shaped(((BLK, HALF), f32), ((HALF, BLK), bf16), ((HALF, BLK), bf16)),
        in_specs=[SM] + [VM] * 7,
        out_specs=[VM] * 3,
        scratch_shapes=[pltpu.VMEM((HALF, BLK), f32)] * 2,
        compiler_params=PARAMS,
        name="grad_full",
    )(flag, q, k, kt, v, do, attn, lse)


def grad_own(q, k, kt, v, do, attn, lse, qseg, kseg, dqt0):
    return pl.pallas_call(
        grad_own_kernel,
        out_shape=shaped(((HALF, BLK), f32), ((HALF, BLK), f32), ((HALF, BLK), f32)),
        in_specs=[VM] * 10,
        out_specs=[VM] * 3,
        scratch_shapes=[pltpu.VMEM((BLK, HALF), f32)],
        compiler_params=PARAMS,
        name="grad_own",
    )(q, k, kt, v, do, attn, lse, qseg, kseg, dqt0)


def positions_of(group_seg):
    token_index = jnp.arange(group_seg.shape[0], dtype=jnp.int32)
    labels = jnp.arange(CONTS + 1, dtype=jnp.int32)
    member = (group_seg[:, None] == labels[None, :]).astype(jnp.int32)
    counts = jnp.sum(member, axis=0)
    starts = jnp.cumsum(counts) - counts
    own_start = jnp.sum(member * starts[None, :], axis=1)
    return token_index - own_start + jnp.where(group_seg > 0, counts[0], 0)


def rope_tables(positions):
    lane = jnp.arange(BLK, dtype=jnp.int32) % 64
    inverse = 10000.0 ** (-2.0 * (lane // 2).astype(f32) / ROT)
    turned = lane < ROT
    phase = positions.astype(f32)[:, None] * jnp.where(turned, inverse, 0.0)[None, :]
    sign = jnp.where(lane % 2 == 0, -1.0, 1.0)
    return jnp.cos(phase), jnp.sin(phase) * sign[None, :]


SWAP = np.zeros((BLK, BLK), np.float32)
for _i in range(BLK):
    SWAP[_i ^ 1, _i] = 1.0


def rope(v, cosine, sine):
    swap = jnp.asarray(SWAP, v.dtype)
    precision = lax.Precision.HIGHEST if v.dtype == f32 else None
    partner = jnp.dot(v, swap, precision=precision, preferred_element_type=f32)
    return v.astype(f32) * cosine + partner * sine


def stats(x):
    average = jnp.mean(x, axis=-1, keepdims=True)
    centred = x - average
    variance = jnp.mean(centred * centred, axis=-1, keepdims=True)
    inv = lax.rsqrt(variance + 1e-05)
    return centred * inv, inv


def gelu(x):
    return jax.nn.gelu(x, approximate=True)


def forward_layer(normed, w, ctx):
    wq, wi, wf, wo, bias_i = w
    cosine, sine, flag, qseg, kseg = ctx
    qkv = jnp.dot(normed, wq, preferred_element_type=f32).astype(bf16)
    k = rope(qkv[:, 128:256], cosine, sine).astype(bf16)
    v = qkv[:, 256:]
    far = lax.ppermute(jnp.concatenate([k, v], 1), "xh", [(0, 1)])
    q = (rope(qkv[:, :128], cosine, sine).astype(bf16).astype(f32) * 0.125).astype(bf16)
    pre = jnp.dot(normed, wi, preferred_element_type=f32) + bias_i
    active = gelu(pre).astype(bf16)
    feed = jnp.dot(active, wf, preferred_element_type=f32)
    acc, m, l = attn_own(q, k, v.T, qseg, kseg)
    k0 = far[:, :128]
    v0 = far[:, 128:]
    attn, lse = attn_full(flag, q, k0, v0.T, acc, m, l)
    branch = jnp.dot(attn, wo, preferred_element_type=f32)
    return scatter_tokens(feed + branch), (normed, q, k, v, k0, v0, attn, lse, pre, active)


def backward_layer(g, gr, w, saved, gain, xhat, inv, ctx):
    wq, wi, wf, wo, bias_i = w
    cosine, sine, flag, qseg, kseg = ctx
    normed, q, k, v, k0, v0, attn, lse, pre, active = saved
    dattn = lax.dot_general(gr, wo, NT, preferred_element_type=f32).astype(bf16)
    dqt0, dk0, dv0 = grad_full(flag, q, k0, k0.T, v0, dattn, attn, lse)
    back = lax.ppermute(jnp.concatenate([dk0, dv0], 1), "xh", [(1, 0)])
    d_active = lax.dot_general(gr, wf, NT, preferred_element_type=f32)
    unused, pull = jax.vjp(gelu, pre)
    d_pre = pull(d_active)[0]
    d_bias_i = jnp.sum(d_pre, axis=0)
    d_pre = d_pre.astype(bf16)
    outer = lambda a, b: lax.dot_general(a, b, (((0,), (0,)), ((), ())), preferred_element_type=f32).astype(bf16)
    g_f = outer(active, gr)
    g_o = outer(attn, gr)
    g_i = outer(normed, d_pre)
    dq, dk, dv = grad_own(q, k, k.T, v, dattn, attn, lse, qseg, kseg, dqt0)
    dk = dk + back[:, :128].astype(f32)
    dv = dv + back[:, 128:].astype(f32)
    d_qkv = jnp.concatenate(
        [rope(dq, cosine, -sine).astype(bf16), rope(dk, cosine, -sine).astype(bf16), dv.astype(bf16)], 1
    )
    g_q = outer(normed, d_qkv)
    partial = lax.dot_general(d_pre, wi, NT, preferred_element_type=f32)
    partial = partial + lax.dot_general(d_qkv, wq, NT, preferred_element_type=f32)
    dn = scatter_tokens(partial)
    d_shift = jnp.sum(dn, axis=0)
    d_gain = jnp.sum(dn * xhat, axis=0)
    dx = dn * gain
    dx = inv * (dx - jnp.mean(dx, -1, keepdims=True) - xhat * jnp.mean(dx * xhat, -1, keepdims=True))
    return g + dx, (g_q, g_i, g_f, g_o, d_bias_i, d_gain, d_shift, jnp.sum(g, axis=0))


ROWS = 144


def transpose_owner(x):
    pairs = [(j * 8 + f, f * 8 + j) for j in range(8) for f in range(8)]
    return lax.ppermute(x, ("y", "core", "z", "xl"), pairs)


def fetch_weights(layer, j, w_qkv, w_out, w_in, b_in, w_fc, small):
    wq = pick(w_qkv[layer].reshape(128, 3, 8, 128), j, 2).reshape(128, 384)
    wi = pick(w_in[layer].reshape(128, 8, 8, 64), j, 2).reshape(128, 512)
    wf = pick(w_fc[layer].reshape(8, 64, D), j, 0).reshape(128, 512)
    wo = transpose_owner(pick(w_out[layer].reshape(8, 16, D), j, 0)).reshape(128, 128)
    body = jnp.concatenate([wq, wi, wf, wo], 1)
    bias = pick(b_in[layer].reshape(8, 64), j, 0)
    row = jnp.concatenate([bias, small])
    row = jnp.pad(row, (0, 1536 - row.shape[0]))[None]
    body = jnp.concatenate([body, jnp.pad(row, ((0, ROWS - 129), (0, 0)))], 0)
    full = lax.all_to_all(jnp.broadcast_to(body[None], (8, ROWS, 1536)), FS, 0, 0, tiled=True)
    main = full[:, :128]
    wq = main[:, :, :384].reshape(D, 384)
    wi = main[:, :, 384:896].reshape(D, 512)
    wf = main[:, :, 896:1408].reshape(512, D)
    wo = main[:, :, 1408:].reshape(128, D)
    bias_i = full[:, 128, :64].reshape(512).astype(f32)
    rest = full[:, 128, 64 : 64 + small.shape[0]]
    return (wq, wi, wf, wo, bias_i), rest


def reduce_layer(grads):
    g_q, g_i, g_f, g_o, d_bias_i, d_gain, d_shift, d_bias_f = grads
    body = jnp.concatenate(
        [
            g_q.reshape(8, 128, 384),
            g_i.reshape(8, 128, 512),
            g_f.reshape(8, 128, 512),
            g_o.reshape(8, 128, 128),
        ],
        2,
    )
    row = jnp.concatenate(
        [d_bias_i.reshape(8, 64), d_gain.reshape(8, 128), d_shift.reshape(8, 128), d_bias_f.reshape(8, 128)], 1
    ).astype(bf16)
    row = jnp.pad(row[:, None], ((0, 0), (0, ROWS - 129), (0, 1536 - 448)))
    body = jnp.concatenate([body, row], 1)
    got = lax.all_to_all(body, FS, 0, 0, tiled=True)
    half = jnp.sum(got.astype(f32), axis=0)
    whole = (half + shift(half.astype(bf16), "xh", 1, 2).astype(f32)).astype(bf16)
    piece = whole[:128, 1408:].reshape(16, D)
    piece = transpose_owner(piece).reshape(128, 128)
    whole = jnp.concatenate([whole[:, :1408], jnp.pad(piece, ((0, ROWS - 128), (0, 0)))], 1)
    y = lax.axis_index("y")
    c = lax.axis_index("core")
    parts = [whole, shift(whole, "y", -1, 4), shift(whole, "y", 2, 4), shift(whole, "y", 1, 4)]
    mine = jnp.stack(parts)
    other = shift(mine, "core", 1, 2)
    pair = jnp.where(c == 0, jnp.stack([mine, other], 1), jnp.stack([other, mine], 1))
    twice = jnp.concatenate([pair, pair], 0)
    allj = lax.dynamic_slice_in_dim(twice, (4 - y) % 4, 4, 0).reshape(8, ROWS, 1536)
    main = allj[:, :128].astype(f32)
    o_q = main[:, :, :384].reshape(8, 128, 3, 128).transpose(1, 2, 0, 3).reshape(128, 3 * D)
    o_i = main[:, :, 384:896].reshape(8, 128, 8, 64).transpose(1, 2, 0, 3).reshape(128, FF)
    o_f = main[:, :, 896:1408].reshape(512, D)
    o_o = main[:, :, 1408:].reshape(128, D)
    rows = allj[:, 128].astype(f32)
    o_bi = rows[:, :64].reshape(512)
    sums = jnp.sum(rows[:, 64:448], axis=0)
    return o_q, o_i, o_f, o_o, o_bi, sums[:128], sums[128:256], sums[256:384]


def body(tokens, segment, ln_gain, ln_bias, w_qkv, w_out, w_in, b_in, w_fc, b_fc, cotangent):
    xh = lax.axis_index("xh")
    j = lax.axis_index("y") * 2 + lax.axis_index("core")
    own = tokens[0]
    all_tokens = gather_tokens(own)
    small = jnp.concatenate([ln_gain.reshape(-1), ln_bias.reshape(-1), b_fc.reshape(-1)])
    w0, rest = fetch_weights(0, j, w_qkv, w_out, w_in, b_in, w_fc, small)
    w1, _ = fetch_weights(1, j, w_qkv, w_out, w_in, b_in, w_fc, small)
    weights = (w0, w1)
    rest = rest.reshape(8, 3, 2, 128).transpose(1, 2, 0, 3).reshape(3, 2, D).astype(f32)
    gain, bias, bias_f = rest[0], rest[1], rest[2]
    gr_top = gather_tokens(cotangent[0])

    group_seg = segment[0]
    positions = positions_of(group_seg)
    start = xh * HALF
    seg = lax.dynamic_slice_in_dim(group_seg, start, HALF, 0)
    cosine, sine = rope_tables(lax.dynamic_slice_in_dim(positions, start, HALF, 0))
    flag = xh.astype(jnp.int32).reshape(1)
    qseg = jnp.broadcast_to(seg[None, :], (8, HALF))
    kseg = jnp.broadcast_to(seg[:, None], (HALF, BLK))
    ctx = (cosine, sine, flag, qseg, kseg)

    x0 = own.astype(f32)
    xhat_all, _ = stats(all_tokens.astype(f32))
    normed0 = (xhat_all * gain[0] + bias[0]).astype(bf16)
    delta0, saved0 = forward_layer(normed0, weights[0], ctx)
    x1 = x0 + delta0 + bias_f[0]
    xhat1, inv1 = stats(x1)
    normed1 = gather_tokens((xhat1 * gain[1] + bias[1]).astype(bf16))
    delta1, saved1 = forward_layer(normed1, weights[1], ctx)
    mixed_out = (x1 + delta1 + bias_f[1]).astype(bf16)

    g2 = cotangent[0].astype(f32)
    g1, grads1 = backward_layer(g2, gr_top, weights[1], saved1, gain[1], xhat1, inv1, ctx)
    out1 = reduce_layer(grads1)
    gr1 = gather_tokens(g1.astype(bf16))
    xhat0, inv0 = stats(x0)
    g0, grads0 = backward_layer(g1, gr1, weights[0], saved0, gain[0], xhat0, inv0, ctx)
    out0 = reduce_layer(grads0)
    o_q, o_i, o_f, o_o, o_bi, o_g, o_s, o_bf = [jnp.stack([a, b]) for a, b in zip(out0, out1)]
    return mixed_out[None], g0[None], o_g, o_s, o_q, o_o, o_i, o_bi, o_f, o_bf


def solution(mesh):
    fine = Mesh(mesh.devices.reshape(2, 4, 2, 4, 2), AXES)
    seq = ("xh", "y", "core")
    tok = P(FS, seq, None)
    two = P(None, FS)
    three = P(None, FS, None)
    in_specs = (tok, P(FS, None), two, two, three, three, three, two, three, two, tok)
    out_specs = (tok, tok, two, two, three, three, three, two, three, two)
    return jax.shard_map(body, mesh=fine, in_specs=in_specs, out_specs=out_specs, check_vma=False)
```

time: 2500 us -> 675 us (0.27)
  waiting for transfers between devices: 1880 us -> 245 us
  blocking collectives: 165 us -> 0 us
  matrix products: 164 us -> 71.5 us
  starting transfers between devices: 61.6 us -> 115 us
  local copies, waits for them, and re-layouts: 92.8 us -> 135 us
  loops' own time: 32.6 us -> 0 us
    reduce_scatter x4 -> x0, waiting for transfers between devices: 863 us -> none  [the longest x1 330 us: reduce_all(): lax.psum_scatter(stacked[6].astype(jnp.bfloat16), 'fsdp', scatter_dimensi...]
    all_gather x8 -> x0, waiting for transfers between devices: 703 us -> none  [the longest x2 286 us: fetch(): lax.all_gather(shards[4][layer_no], 'fsdp', axis=0, tiled=True)]
    ppermute x0 -> x50, waiting for transfers between devices: none -> 245 us  [the longest x42 165 us: shift(): return lax.ppermute(x, axis, [(i, (i + by) % size) for i in range(size)])]
    unnamed x21 -> x0, waiting for transfers between devices: 134 us -> none
    all_gather x8 -> x0, blocking collectives: 126 us -> none  [the longest x2 42 us: fetch(): lax.all_gather(shards[5][layer_no], 'fsdp', axis=0, tiled=True)]
    psum x1 -> x0, waiting for transfers between devices: 121 us -> none  [reduce_all(): lax.psum(owned[2].astype(jnp.bfloat16), 'seq').astype(jnp.float32)]
    dot_general x80 -> x32, matrix products: 164 us -> 71.5 us  [the longest x8 19.7 us: rope(): partner = jnp.dot(v, swap, precision=precision, preferred_element_type=f32)]
    ppermute x0 -> x50, starting transfers between devices: none -> 90.9 us  [the longest x42 51.2 us: shift(): return lax.ppermute(x, axis, [(i, (i + by) % size) for i in range(size)])]
  transfers between devices with their start and end apart: 25 -> 54, of which waited for: 20 -> 36; matrix products, arithmetic and copies ran while one was open for 12% -> 27% of each run, Pallas kernels for 0% -> 3%
where the time goes in v1:
time: 675 us; the launch traced here: 666 us
  waiting for transfers between devices  245 us (36%)
  local copies, waits for them, and re-layouts  135 us (20%)
  starting transfers between devices  115 us (17%)
  other arithmetic  78.7 us (12%)
  matrix products  71.5 us (11%)
  Pallas kernels  18 us (3%)
    ppermute x42, waiting for transfers between devices, shift(): return lax.ppermute(x, axis, [(i, (i + by) % size) for i in range(size)])  165 us
    ppermute x42, starting transfers between devices, shift(): return lax.ppermute(x, axis, [(i, (i + by) % size) for i in range(size)])  51.2 us
    ppermute x2, waiting for transfers between devices, backward_layer(): back = lax.ppermute(jnp.concatenate([dk0, dv0], 1), 'xh', [(1, 0)])  41.6 us
    unnamed x205, local copies, waits for them, and re-layouts  32.8 us
    ppermute x4, waiting for transfers between devices, transpose_owner(): return lax.ppermute(x, ('y', 'core', 'z', 'xl'), pairs)  21.3 us
    dot_general x8, matrix products, rope(): partner = jnp.dot(v, swap, precision=precision, preferred_element_type=f32)  19.7 us
    ppermute x2, waiting for transfers between devices, forward_layer(): far = lax.ppermute(jnp.concatenate([k, v], 1), 'xh', [(0, 1)])  17.3 us
    ppermute x2, starting transfers between devices, forward_layer(): far = lax.ppermute(jnp.concatenate([k, v], 1), 'xh', [(0, 1)])  17.2 us
  transfers between devices with their start and end apart: 54, of which 36 were waited for; matrix products, arithmetic and copies ran while one was open for 27% of the time, Pallas kernels for 3%

profile of v1, /device:TPU:1, one launch (start us, length us, event | category | flops | bytes accessed | tf_op | source)
XLA Modules:
  0.0 666.4 jit_solution(15288180221840912698)
XLA Ops:
  21.4 6.7 %all-to-all-start = ((bf16[8,144,1536]{2,1,0:T(8,128)(2,1)}), bf16[8,144,1536]{2,1,0:T(8,128)(2,1)}, u32[]{:S(2)}, u32[]{:S(2)}) async-start(bf16[8,144,1536]{2,1,0:T(8,128)(2,1)} %broadcast_in_dim.37), calls=%async_computation | async-start | bytes 7077888 | tf_op jit(solution)/shard_map/all_to_all | solution.py:382
  33.6 5.1 collective-permute-done.1
  38.6 6.5 collective-permute-done
  50.8 19.9 %collective-permute-done.14 = bf16[16,1024]{1,0:T(8,128)(2,1)S(1)} collective-permute-done((bf16[16,1024]{1,0:T(8,128)(2,1)S(1)}, bf16[16,1024]{1,0:T(8,128)(2,1)S(1)}, u32[]{:S(2)}, u32[]{:S(2)}) %collective-permute-start.14) | collective-permute-done | bytes 32800 | tf_op jit(solution)/shard_map/ppermute | solution.py:369
  76.9 7.4 %all-to-all-start.1 = ((bf16[8,144,1536]{2,1,0:T(8,128)(2,1)}), bf16[8,144,1536]{2,1,0:T(8,128)(2,1)}, u32[]{:S(2)}, u32[]{:S(2)}) async-start(bf16[8,144,1536]{2,1,0:T(8,128)(2,1)} %broadcast_in_dim.46), calls=%async_computation.1 | async-start | bytes 7077888 | tf_op jit(solution)/shard_map/all_to_all | solution.py:382
  98.8 5.3 collective-permute-start.5
  111.7 5.4 fusion.125
  117.1 17.3 %collective-permute-done.5 = bf16[1024,256]{1,0:T(8,128)(2,1)} collective-permute-done((bf16[1024,256]{1,0:T(8,128)(2,1)}, bf16[1024,256]{1,0:T(8,128)(2,1)}, u32[]{:S(2)}, u32[]{:S(2)}) %collective-permute-start.5) | collective-permute-done | bytes 524320 | tf_op jit(solution)/shard_map/ppermute | solution.py:318
  144.2 6.7 %collective-permute-done.21 = bf16[128,1024]{1,0:T(8,128)(2,1)S(1)} collective-permute-done((bf16[128,1024]{1,0:T(8,128)(2,1)S(1)}, bf16[128,1024]{1,0:T(8,128)(2,1)S(1)}, u32[]{:S(2)}, u32[]{:S(2)}) %collective-permute-start.21) | collective-permute-done | bytes 262176 | tf_op jit(solution)/shard_map/ppermute | solution.py:27
  218.8 12.0 %collective-permute-start.15 = (bf16[1024,256]{1,0:T(8,128)(2,1)}, bf16[1024,256]{1,0:T(8,128)(2,1)}, u32[]{:S(2)}, u32[]{:S(2)}) collective-permute-start(bf16[1024,256]{1,0:T(8,128)(2,1)} %pad_maximum_fusion.13), channel_id=1, source_target_pairs={{0,64},{1,65},{2,66},{3,67},{4,68},{5,69},{6,70},{7,71},{8,72},{9,... | collective-permute-start | bytes 1572872 | tf_op jit(solution)/shard_map/ppermute | solution.py:318
  243.7 5.5 fusion.126
  258.3 6.4 collective-permute-start.24
  272.9 9.3 %collective-permute-done.24 = bf16[1024,256]{1,0:T(8,128)(2,1)S(1)} collective-permute-done((bf16[1024,256]{1,0:T(8,128)(2,1)S(1)}, bf16[1024,256]{1,0:T(8,128)(2,1)S(1)}, u32[]{:S(2)}, u32[]{:S(2)}) %collective-permute-start.24) | collective-permute-done | bytes 524320 | tf_op jit(solution)/shard_map/ppermute | solution.py:337
  336.1 6.0 collective-permute-done.30
  354.6 5.5 all-to-all-start.3
  378.2 32.3 %collective-permute-done.33 = bf16[1024,256]{1,0:T(8,128)(2,1)S(1)} collective-permute-done((bf16[1024,256]{1,0:T(8,128)(2,1)S(1)}, bf16[1024,256]{1,0:T(8,128)(2,1)S(1)}, u32[]{:S(2)}, u32[]{:S(2)}) %collective-permute-start.33) | collective-permute-done | bytes 524320 | tf_op jit(solution)/shard_map/ppermute | solution.py:337
  455.8 45.4 %collective-permute-done.44 = bf16[144,1536]{1,0:T(8,128)(2,1)S(1)} collective-permute-done((bf16[144,1536]{1,0:T(8,128)(2,1)S(1)}, bf16[144,1536]{1,0:T(8,128)(2,1)S(1)}, u32[]{:S(2)}, u32[]{:S(2)}) %collective-permute-start.44) | collective-permute-done | bytes 442400 | tf_op jit(solution)/shard_map/ppermute | solution.py:27
  513.0 5.4 collective-permute-start.47
  519.9 8.1 %collective-permute-done.47 = bf16[144,1536]{1,0:T(8,128)(2,1)S(1)} collective-permute-done((bf16[144,1536]{1,0:T(8,128)(2,1)S(1)}, bf16[144,1536]{1,0:T(8,128)(2,1)S(1)}, u32[]{:S(2)}, u32[]{:S(2)}) %collective-permute-start.47) | collective-permute-done | bytes 442400 | tf_op jit(solution)/shard_map/ppermute | solution.py:27
  528.0 9.0 %collective-permute-done.46 = bf16[144,1536]{1,0:T(8,128)(2,1)S(1)} collective-permute-done((bf16[144,1536]{1,0:T(8,128)(2,1)S(1)}, bf16[144,1536]{1,0:T(8,128)(2,1)S(1)}, u32[]{:S(2)}, u32[]{:S(2)}) %collective-permute-start.46) | collective-permute-done | bytes 442400 | tf_op jit(solution)/shard_map/ppermute | solution.py:27
  546.6 9.5 %collective-permute-done.38 = bf16[144,1536]{1,0:T(8,128)(2,1)S(1)} collective-permute-done((bf16[144,1536]{1,0:T(8,128)(2,1)S(1)}, bf16[144,1536]{1,0:T(8,128)(2,1)S(1)}, u32[]{:S(2)}, u32[]{:S(2)}) %collective-permute-start.38) | collective-permute-done | bytes 442400 | tf_op jit(solution)/shard_map/ppermute | solution.py:27
  563.3 7.8 %collective-permute-start.41 = (bf16[144,1536]{1,0:T(8,128)(2,1)}, bf16[144,1536]{1,0:T(8,128)(2,1)}, u32[]{:S(2)}, u32[]{:S(2)}) collective-permute-start(bf16[144,1536]{1,0:T(8,128)(2,1)} %get-tuple-element.188), channel_id=1, source_target_pairs={{0,32},{16,48},{32,0},{48,16},{1,33},{17,49},{33,1},{49,17},{2,34}... | collective-permute-start | bytes 1327112 | tf_op jit(solution)/shard_map/ppermute | solution.py:27
  583.7 6.2 collective-permute-done.40
  654.8 5.8 copy.283
  (538 shorter events, 409.4 us)
Async XLA Ops:
  1.7 17.0 %collective-permute-start.4 = (bf16[16,1024]{1,0:T(8,128)(2,1)S(1)}, bf16[16,1024]{1,0:T(8,128)(2,1)S(1)}, u32[]{:S(2)}, u32[]{:S(2)}) collective-permute-start(bf16[16,1024]{1,0:T(8,128)(2,1)S(1)} %dynamic-slice_bitcast_fusion.13), channel_id=1, source_target_pairs={{0,0},{1,8},{2,16},{3,24},{4,32},{5,40},{6,48},{7,56},{8,1},{9,9},... | collective-permute-start | bytes 98312 | tf_op jit(solution)/shard_map/ppermute | solution.py:369
  21.4 53.4 %all-to-all-start = ((bf16[8,144,1536]{2,1,0:T(8,128)(2,1)}), bf16[8,144,1536]{2,1,0:T(8,128)(2,1)}, u32[]{:S(2)}, u32[]{:S(2)}) async-start(bf16[8,144,1536]{2,1,0:T(8,128)(2,1)} %broadcast_in_dim.37), calls=%async_computation | async-start | bytes 7077888 | tf_op jit(solution)/shard_map/all_to_all | solution.py:382
  46.3 25.0 %collective-permute-start.3 = (bf16[4,128,1024]{2,1,0:T(8,128)(2,1)}, bf16[4,128,1024]{2,1,0:T(8,128)(2,1)}, u32[]{:S(2)}, u32[]{:S(2)}) collective-permute-start(bf16[4,128,1024]{2,1,0:T(8,128)(2,1)} %get-tuple-element.171), channel_id=1, source_target_pairs={{0,8},{8,0},{1,9},{9,1},{2,10},{10,2},{3,11},{11,3},{4,12},{12,4},... | collective-permute-start | bytes 3145736 | tf_op jit(solution)/shard_map/ppermute | solution.py:27
  46.5 24.2 %collective-permute-start.14 = (bf16[16,1024]{1,0:T(8,128)(2,1)S(1)}, bf16[16,1024]{1,0:T(8,128)(2,1)S(1)}, u32[]{:S(2)}, u32[]{:S(2)}) collective-permute-start(bf16[16,1024]{1,0:T(8,128)(2,1)S(1)} %dynamic-slice_bitcast_fusion.12), channel_id=1, source_target_pairs={{0,0},{1,8},{2,16},{3,24},{4,32},{5,40},{6,48},{7,56},{8,1},{9,9},... | collective-permute-start | bytes 98312 | tf_op jit(solution)/shard_map/ppermute | solution.py:369
  76.9 104.5 %all-to-all-start.1 = ((bf16[8,144,1536]{2,1,0:T(8,128)(2,1)}), bf16[8,144,1536]{2,1,0:T(8,128)(2,1)}, u32[]{:S(2)}, u32[]{:S(2)}) async-start(bf16[8,144,1536]{2,1,0:T(8,128)(2,1)} %broadcast_in_dim.46), calls=%async_computation.1 | async-start | bytes 7077888 | tf_op jit(solution)/shard_map/all_to_all | solution.py:382
  98.8 35.5 %collective-permute-start.5 = (bf16[1024,256]{1,0:T(8,128)(2,1)}, bf16[1024,256]{1,0:T(8,128)(2,1)}, u32[]{:S(2)}, u32[]{:S(2)}) collective-permute-start(bf16[1024,256]{1,0:T(8,128)(2,1)} %pad_maximum_fusion.12), channel_id=1, source_target_pairs={{0,64},{1,65},{2,66},{3,67},{4,68},{5,69},{6,70},{7,71},{8,72},{9,... | collective-permute-start | bytes 1572872 | tf_op jit(solution)/shard_map/ppermute | solution.py:318
  140.9 18.1 %collective-permute-start.6 = (bf16[4,128,1024]{2,1,0:T(8,128)(2,1)}, bf16[4,128,1024]{2,1,0:T(8,128)(2,1)}, u32[]{:S(2)}, u32[]{:S(2)}) collective-permute-start(bf16[4,128,1024]{2,1,0:T(8,128)(2,1)} %fusion.46), channel_id=1, source_target_pairs={{0,8},{8,0},{1,9},{9,1},{2,10},{10,2},{3,11},{11,3},{4,12},{12,4},... | collective-permute-start | bytes 3145736 | tf_op jit(solution)/shard_map/ppermute | solution.py:27
  218.8 30.4 %collective-permute-start.15 = (bf16[1024,256]{1,0:T(8,128)(2,1)}, bf16[1024,256]{1,0:T(8,128)(2,1)}, u32[]{:S(2)}, u32[]{:S(2)}) collective-permute-start(bf16[1024,256]{1,0:T(8,128)(2,1)} %pad_maximum_fusion.13), channel_id=1, source_target_pairs={{0,64},{1,65},{2,66},{3,67},{4,68},{5,69},{6,70},{7,71},{8,72},{9,... | collective-permute-start | bytes 1572872 | tf_op jit(solution)/shard_map/ppermute | solution.py:318
  258.3 23.9 %collective-permute-start.24 = (bf16[1024,256]{1,0:T(8,128)(2,1)S(1)}, bf16[1024,256]{1,0:T(8,128)(2,1)S(1)}, u32[]{:S(2)}, u32[]{:S(2)}) collective-permute-start(bf16[1024,256]{1,0:T(8,128)(2,1)S(1)} %pad_maximum_fusion.14), channel_id=1, source_target_pairs={{64,0},{65,1},{66,2},{67,3},{68,4},{69,5},{70,6},{71,7},{72,8},{73... | collective-permute-start | bytes 1572872 | tf_op jit(solution)/shard_map/ppermute | solution.py:337
  308.0 16.5 %collective-permute-start.17 = (bf16[128,1024]{1,0:T(8,128)(2,1)S(1)}, bf16[128,1024]{1,0:T(8,128)(2,1)S(1)}, u32[]{:S(2)}, u32[]{:S(2)}) collective-permute-start(bf16[128,1024]{1,0:T(8,128)(2,1)S(1)} %get-tuple-element.162), channel_id=1, source_target_pairs={{0,32},{16,48},{32,0},{48,16},{1,33},{17,49},{33,1},{49,17},{2,34}... | collective-permute-start | bytes 786440 | tf_op jit(solution)/shard_map/ppermute | solution.py:27
  309.9 18.8 %collective-permute-start.19 = (bf16[128,1024]{1,0:T(8,128)(2,1)S(1)}, bf16[128,1024]{1,0:T(8,128)(2,1)S(1)}, u32[]{:S(2)}, u32[]{:S(2)}) collective-permute-start(bf16[128,1024]{1,0:T(8,128)(2,1)S(1)} %get-tuple-element.163), channel_id=1, source_target_pairs={{0,48},{16,0},{32,16},{48,32},{1,49},{17,1},{33,17},{49,33},{2,50}... | collective-permute-start | bytes 786440 | tf_op jit(solution)/shard_map/ppermute | solution.py:27
  313.2 17.7 %collective-permute-start.18 = (bf16[128,1024]{1,0:T(8,128)(2,1)S(1)}, bf16[128,1024]{1,0:T(8,128)(2,1)S(1)}, u32[]{:S(2)}, u32[]{:S(2)}) collective-permute-start(bf16[128,1024]{1,0:T(8,128)(2,1)S(1)} %get-tuple-element.164), channel_id=1, source_target_pairs={{0,16},{16,32},{32,48},{48,0},{1,17},{17,33},{33,49},{49,1},{2,18}... | collective-permute-start | bytes 786440 | tf_op jit(solution)/shard_map/ppermute | solution.py:27
  354.6 93.8 %all-to-all-start.3 = ((bf16[8,144,1536]{2,1,0:T(8,128)(2,1)}), bf16[8,144,1536]{2,1,0:T(8,128)(2,1)}, u32[]{:S(2)}, u32[]{:S(2)}) async-start(bf16[8,144,1536]{2,1,0:T(8,128)(2,1)} %fusion.9), calls=%async_computation.3 | async-start | bytes 7077888 | tf_op jit(solution)/shard_map/all_to_all | solution.py:409
  368.6 41.8 %collective-permute-start.33 = (bf16[1024,256]{1,0:T(8,128)(2,1)S(1)}, bf16[1024,256]{1,0:T(8,128)(2,1)S(1)}, u32[]{:S(2)}, u32[]{:S(2)}) collective-permute-start(bf16[1024,256]{1,0:T(8,128)(2,1)S(1)} %pad_maximum_fusion.15), channel_id=1, source_target_pairs={{64,0},{65,1},{66,2},{67,3},{68,4},{69,5},{70,6},{71,7},{72,8},{73... | collective-permute-start | bytes 1572872 | tf_op jit(solution)/shard_map/ppermute | solution.py:337
  448.4 92.8 %all-to-all-start.2 = ((bf16[8,144,1536]{2,1,0:T(8,128)(2,1)}), bf16[8,144,1536]{2,1,0:T(8,128)(2,1)S(1)}, u32[]{:S(2)}, u32[]{:S(2)}) async-start(bf16[8,144,1536]{2,1,0:T(8,128)(2,1)} %fusion.8), calls=%async_computation.2 | async-start | bytes 7077888 | tf_op jit(solution)/shard_map/all_to_all | solution.py:409
  455.7 45.4 %collective-permute-start.44 = (bf16[144,1536]{1,0:T(8,128)(2,1)S(1)}, bf16[144,1536]{1,0:T(8,128)(2,1)S(1)}, u32[]{:S(2)}, u32[]{:S(2)}) collective-permute-start(bf16[144,1536]{1,0:T(8,128)(2,1)S(1)} %convert_element_type.444), channel_id=1, source_target_pairs={{0,64},{64,0},{1,65},{65,1},{2,66},{66,2},{3,67},{67,3},{4,68},{68... | collective-permute-start | bytes 1327112 | tf_op jit(solution)/shard_map/ppermute | solution.py:27
  513.0 15.0 %collective-permute-start.47 = (bf16[144,1536]{1,0:T(8,128)(2,1)S(1)}, bf16[144,1536]{1,0:T(8,128)(2,1)S(1)}, u32[]{:S(2)}, u32[]{:S(2)}) collective-permute-start(bf16[144,1536]{1,0:T(8,128)(2,1)S(1)} %get-tuple-element.190), channel_id=1, source_target_pairs={{0,32},{16,48},{32,0},{48,16},{1,33},{17,49},{33,1},{49,17},{2,34}... | collective-permute-start | bytes 1327112 | tf_op jit(solution)/shard_map/ppermute | solution.py:27
  518.5 18.5 %collective-permute-start.46 = (bf16[144,1536]{1,0:T(8,128)(2,1)S(1)}, bf16[144,1536]{1,0:T(8,128)(2,1)S(1)}, u32[]{:S(2)}, u32[]{:S(2)}) collective-permute-start(bf16[144,1536]{1,0:T(8,128)(2,1)S(1)} %get-tuple-element.190), channel_id=1, source_target_pairs={{0,48},{16,0},{32,16},{48,32},{1,49},{17,1},{33,17},{49,33},{2,50}... | collective-permute-start | bytes 1327112 | tf_op jit(solution)/shard_map/ppermute | solution.py:27
  518.5 20.1 %collective-permute-start.48 = (bf16[144,1536]{1,0:T(8,128)(2,1)S(1)}, bf16[144,1536]{1,0:T(8,128)(2,1)S(1)}, u32[]{:S(2)}, u32[]{:S(2)}) collective-permute-start(bf16[144,1536]{1,0:T(8,128)(2,1)S(1)} %get-tuple-element.190), channel_id=1, source_target_pairs={{0,16},{16,32},{32,48},{48,0},{1,17},{17,33},{33,49},{49,1},{2,18}... | collective-permute-start | bytes 1327112 | tf_op jit(solution)/shard_map/ppermute | solution.py:27
  540.6 32.2 %collective-permute-start.49 = (bf16[4,144,1536]{2,1,0:T(8,128)(2,1)}, bf16[4,144,1536]{2,1,0:T(8,128)(2,1)}, u32[]{:S(2)}, u32[]{:S(2)}) collective-permute-start(bf16[4,144,1536]{2,1,0:T(8,128)(2,1)} %get-tuple-element.149), channel_id=1, source_target_pairs={{0,8},{8,0},{1,9},{9,1},{2,10},{10,2},{3,11},{11,3},{4,12},{12,4},... | collective-permute-start | bytes 5308424 | tf_op jit(solution)/shard_map/ppermute | solution.py:27
  563.3 20.4 %collective-permute-start.41 = (bf16[144,1536]{1,0:T(8,128)(2,1)}, bf16[144,1536]{1,0:T(8,128)(2,1)}, u32[]{:S(2)}, u32[]{:S(2)}) collective-permute-start(bf16[144,1536]{1,0:T(8,128)(2,1)} %get-tuple-element.188), channel_id=1, source_target_pairs={{0,32},{16,48},{32,0},{48,16},{1,33},{17,49},{33,1},{49,17},{2,34}... | collective-permute-start | bytes 1327112 | tf_op jit(solution)/shard_map/ppermute | solution.py:27
  571.0 18.9 %collective-permute-start.40 = (bf16[144,1536]{1,0:T(8,128)(2,1)}, bf16[144,1536]{1,0:T(8,128)(2,1)}, u32[]{:S(2)}, u32[]{:S(2)}) collective-permute-start(bf16[144,1536]{1,0:T(8,128)(2,1)} %get-tuple-element.188), channel_id=1, source_target_pairs={{0,48},{16,0},{32,16},{48,32},{1,49},{17,1},{33,17},{49,33},{2,50}... | collective-permute-start | bytes 1327112 | tf_op jit(solution)/shard_map/ppermute | solution.py:27
  571.0 20.4 %collective-permute-start.42 = (bf16[144,1536]{1,0:T(8,128)(2,1)}, bf16[144,1536]{1,0:T(8,128)(2,1)}, u32[]{:S(2)}, u32[]{:S(2)}) collective-permute-start(bf16[144,1536]{1,0:T(8,128)(2,1)} %get-tuple-element.188), channel_id=1, source_target_pairs={{0,16},{16,32},{32,48},{48,0},{1,17},{17,33},{33,49},{49,1},{2,18}... | collective-permute-start | bytes 1327112 | tf_op jit(solution)/shard_map/ppermute | solution.py:27
  595.2 20.2 %collective-permute-start.43 = (bf16[4,144,1536]{2,1,0:T(8,128)(2,1)}, bf16[4,144,1536]{2,1,0:T(8,128)(2,1)}, u32[]{:S(2)}, u32[]{:S(2)}) collective-permute-start(bf16[4,144,1536]{2,1,0:T(8,128)(2,1)} %get-tuple-element.147), channel_id=1, source_target_pairs={{0,8},{8,0},{1,9},{9,1},{2,10},{10,2},{3,11},{11,3},{4,12},{12,4},... | collective-permute-start | bytes 5308424 | tf_op jit(solution)/shard_map/ppermute | solution.py:27
  (130 other events, 1951.9 us)

commit v2 on v1

v2 whole, which is shorter than its diff:
```python
import functools
import jax
import jax.numpy as jnp
from jax import lax
from jax.experimental import pallas as pl
from jax.experimental.pallas import tpu as pltpu
from jax.sharding import Mesh, PartitionSpec as P

ROT = 32
CONTS = 8
D = 1024
HALF = 1024
BLK = 128
QB = 256
AXES = ("xh", "y", "core", "z", "xl")
FS = ("z", "xl")
f32 = jnp.float32
bf16 = jnp.bfloat16
NT = (((1,), (1,)), ((), ()))
VM = pl.BlockSpec(memory_space=pltpu.VMEM)
SM = pl.BlockSpec(memory_space=pltpu.SMEM)
ANY = pl.BlockSpec(memory_space=pl.ANY)
HBM = pl.BlockSpec(memory_space=pltpu.HBM)
MB = 1024 * 1024


def sds(*args):
    return [jax.ShapeDtypeStruct(s, t) for s, t in args]


class Far:
    def __init__(self, ref, copy):
        self.ref, self.copy = ref, copy

    def here(self):
        if self.copy is not None:
            self.copy.wait()
            self.copy = None
        return self.ref

    def __getitem__(self, index):
        return self.here()[index]

    @property
    def shape(self):
        return self.ref.shape


class Out:
    def __init__(self, ref, copy):
        self.ref, self.copy, self.sent = ref, copy, False

    def __getitem__(self, index):
        return self.ref[index]

    def __setitem__(self, index, value):
        self.ref[index] = value

    @property
    def dtype(self):
        return self.ref.dtype

    @property
    def shape(self):
        return self.ref.shape

    def send(self):
        self.copy.start()
        self.sent = True


COST = 0.001
LIMIT = 51


def call(kernel, name, outs, args, us, scratch=(), limit=None, after=(), raw=(), vm=(), out_raw=(), out_vm=(), alias=None):
    n, m = len(args), len(outs)
    fetched = [i for i in range(1, n) if i not in raw and i not in vm]
    staged = [i for i in range(m) if i not in out_raw and i not in out_vm]

    def run(*refs):
        ins = list(refs[:n])
        results = list(refs[n + len(after) : n + len(after) + m])
        rest = list(refs[n + len(after) + m :])
        own, rest = rest[: len(scratch)], rest[len(scratch) :]
        sems = rest[-1]
        copies = []
        for k, i in enumerate(fetched):
            copy = pltpu.make_async_copy(ins[i], rest[k], sems.at[k])
            copies.append(copy)
            ins[i] = Far(rest[k], copy)
        for copy in copies:
            copy.start()
        for k, i in enumerate(staged):
            ref = rest[len(fetched) + k]
            results[i] = Out(ref, pltpu.make_async_copy(ref, results[i], sems.at[len(fetched) + k]))
        kernel(*ins, *results, *own)
        for i in fetched:
            ins[i].here()
        for i in staged:
            if not results[i].sent:
                results[i].send()
        for i in staged:
            results[i].copy.wait()

    room = [pltpu.VMEM(args[i].shape, args[i].dtype) for i in fetched]
    room += [pltpu.VMEM(outs[i][0], outs[i][1]) for i in staged]
    return pl.pallas_call(
        run,
        out_shape=sds(*outs),
        in_specs=[SM] + [VM if i in vm else HBM for i in range(1, n)] + [ANY] * len(after),
        out_specs=[VM if i in out_vm else HBM for i in range(m)],
        scratch_shapes=list(scratch) + room + [pltpu.SemaphoreType.DMA((max(1, len(room)),))],
        input_output_aliases=alias or {},
        compiler_params=pltpu.CompilerParams(vmem_limit_bytes=(limit or LIMIT) * MB),
        cost_estimate=pl.CostEstimate(flops=int(us * COST * 1e9), bytes_accessed=int(us * COST * 1e6), transcendentals=0),
        name=name,
    )(*args, *after)


def dma(n):
    return pltpu.SemaphoreType.DMA((n,))


def copy_all(pairs, sems):
    copies = [pltpu.make_async_copy(a, b, sems.at[i]) for i, (a, b) in enumerate(pairs)]
    for copy in copies:
        copy.start()
    return copies


def wait_all(copies):
    for copy in copies:
        copy.wait()


def shift(x, axis, by, size):
    return lax.ppermute(x, axis, [(i, (i + by) % size) for i in range(size)])


def gather_blocks(own, hold=None):
    one = shift(own, "y", -1, 4)
    three = shift(own, "y", 1, 4)
    two = shift(own, "y", 2, 4)
    if hold is not None:
        one, two, three = hold(one, two, three)
    blocks = []
    for mine in (own, one, two, three):
        blocks += [mine, shift(mine, "core", 1, 2)]
    return blocks


def spread(low):
    return [shift(low[r - 1], "y", r, 4) for r in (1, 2, 3)]


def transpose_owner(x):
    pairs = [(j * 8 + f, f * 8 + j) for j in range(8) for f in range(8)]
    return lax.ppermute(x, ("y", "core", "z", "xl"), pairs)


def gate(ids, x, after):
    (out,) = call(lambda *refs: None, "gate", [(x.shape, x.dtype)], (ids, x), 1, raw=(1,), out_raw=(0,), after=after, alias={1: 0})
    return out


def gate_all(ids, xs, after):
    n = len(xs)
    return call(
        lambda *refs: None, "gate", [(x.shape, x.dtype) for x in xs], (ids, *xs), 1, raw=range(1, n + 1), out_raw=range(n),
        after=after, alias={i + 1: i for i in range(n)},
    )


def gather_fsdp(ids, x, got, after=()):
    (pair,) = call(
        pair_kernel, "pair", [((2,) + x.shape, bf16)], (ids, x, got), 2, [dma(2)], out_raw=(0,), after=after, limit=62,
    )
    return [pair, shift(pair, "z", -1, 4), shift(pair, "z", 2, 4), shift(pair, "z", 1, 4)]


def weight_copies(ids, pairs, cols, room):
    if len(pairs) == 1:
        return [(pairs[0].at[:, :, cols], room)]
    out = []
    for r in range(4):
        out.append((pairs[r].at[:, :, cols], room.at[pl.ds(2 * lax.rem(ids[4] + r, 4), 2)]))
    return out


def slot(ids, r, s):
    y = lax.rem(ids[0] + r, 4)
    c = ids[1] if s == 0 else 1 - ids[1]
    return y * 2 + c


def rows_of(ids, r, s, n=BLK):
    return pl.ds(pl.multiple_of(slot(ids, r, s) * n, n), n)


def turn(v, cosine, sine):
    lane = lax.broadcasted_iota(jnp.int32, v.shape, 1)
    partner = jnp.where(lane % 2 == 0, pltpu.roll(v, BLK - 1, 1), pltpu.roll(v, 1, 1))
    return v * cosine + partner * sine


def stats(x):
    average = jnp.mean(x, axis=-1, keepdims=True)
    centred = x - average
    variance = jnp.mean(centred * centred, axis=-1, keepdims=True)
    inv = lax.rsqrt(variance + 1e-05)
    return centred * inv, inv


def gelu_both(x):
    a = 0.7978845608028654
    b = 0.044715
    sq = x * x
    t = jnp.tanh(a * x * (1.0 + b * sq))
    half = 0.5 * (1.0 + t)
    slope = half + 0.5 * x * (1.0 - t * t) * a * (1.0 + 3.0 * b * sq)
    return x * half, slope


def dot(a, b):
    return jnp.dot(a, b, preferred_element_type=f32)


def dot_nt(a, b):
    return lax.dot_general(a, b, NT, preferred_element_type=f32)


def pack_q_kernel(ids, wq, gain, bias, bfc, bin_, q0, room, small, binv, sems, out_sems):
    j = ids[0] * 2 + ids[1]
    pairs = []
    for part in range(3):
        cols = pl.ds(pl.multiple_of(part * D + j * BLK, BLK), BLK)
        pairs.append((wq.at[0, :, cols], room.at[0:BLK, part * BLK : part * BLK + BLK]))
    pairs += [(ref, small.at[i]) for i, ref in enumerate((gain, bias, bfc))]
    pairs.append((bin_, binv))
    wait_all(copy_all(pairs, sems))
    chunk = binv[:, pl.ds(pl.multiple_of((j // 2) * BLK, BLK), BLK)].astype(f32)
    chunk = jnp.where(j % 2 == 1, pltpu.roll(chunk, 64, 1), chunk)
    lane = lax.broadcasted_iota(jnp.int32, (1, BLK), 1)
    row2 = jnp.where(lane < 64, chunk[0:1], pltpu.roll(chunk, 64, 1)[1:2])
    blank = jnp.zeros((13, BLK), f32)
    cols = [jnp.concatenate([small[i].astype(f32), row2, blank], 0) for i in range(3)]
    room[BLK:, :] = jnp.concatenate(cols, 1).astype(bf16)
    wait_all(copy_all([(room, q0.at[f]) for f in range(8)], out_sems))


def pack_layer(layer, ids, wi, wf, out, chunks, sems, more=()):
    j = ids[0] * 2 + ids[1]
    rows = pl.ds(pl.multiple_of(j * 64, 64), 64)
    pairs = []
    for f in range(8):
        cols = pl.ds(pl.multiple_of(f * 512 + (j // 2) * BLK, BLK), BLK)
        pairs.append((wi.at[layer, :, cols], chunks.at[f]))
    pairs.append((wf.at[layer, rows, 0:512], out.ref.at[0:64, 512:1024]))
    pairs.append((wf.at[layer, rows, 512:1024], out.ref.at[64:128, 512:1024]))
    wait_all(copy_all(pairs + list(more), sems))
    lane = lax.broadcasted_iota(jnp.int32, (BLK, BLK), 1)
    odd = j % 2 == 1
    for pair in range(4):
        a = chunks[2 * pair].astype(f32)
        b = chunks[2 * pair + 1].astype(f32)
        first = jnp.where(odd, pltpu.roll(a, 64, 1), a)
        second = jnp.where(odd, b, pltpu.roll(b, 64, 1))
        out[:, pair * BLK : pair * BLK + BLK] = jnp.where(lane < 64, first, second).astype(bf16)


def pack_first_kernel(ids, wi, wf, out, chunks, sems):
    pack_layer(0, ids, wi, wf, out, chunks, sems)


def pack_second_kernel(ids, wi, wf, wq, out, chunks, sems):
    j = ids[0] * 2 + ids[1]
    more = []
    for part in range(3):
        cols = pl.ds(pl.multiple_of(part * D + j * BLK, BLK), BLK)
        more.append((wq.at[1, :, cols], out.ref.at[:, D + part * BLK : D + part * BLK + BLK]))
    pack_layer(1, ids, wi, wf, out, chunks, sems, more)


def pass_kernel(layer, ids, x, out, sems):
    wait_all(copy_all([(x.at[layer], out.ref)], sems))


def join_kernel(ids, a, b, out, sems):
    wait_all(copy_all([(a, out.ref.at[0:BLK]), (b, out.ref.at[BLK : 2 * BLK])], sems))


def pair_kernel(ids, own, got, out, sems):
    xl = ids[3]
    wait_all(copy_all([(own.here(), out.at[xl]), (got.here(), out.at[1 - xl])], sems))


def four_kernel(ids, own, got, out, sems):
    xl = ids[3]
    mine, other = own.here(), got.here()
    wait_all(copy_all([(src, out.at[z, at]) for z in range(4) for src, at in ((mine, xl), (other, 1 - xl))], sems))


def params_part(rows_of_f, gain, bias, bfc, bi):
    lane = lax.broadcasted_iota(jnp.int32, (1, BLK), 1)
    for f in range(8):
        cols = slice(f * BLK, f * BLK + BLK)
        rows = rows_of_f[f].astype(f32)
        gain[:, cols] = rows[0:2, 0:BLK]
        bias[:, cols] = rows[0:2, BLK : 2 * BLK]
        bfc[:, cols] = rows[0:2, 2 * BLK :]
    for pair in range(4):
        a = rows_of_f[2 * pair].astype(f32)[2:3, :BLK]
        b = rows_of_f[2 * pair + 1].astype(f32)[2:3, :BLK]
        cols = slice(pair * BLK, pair * BLK + BLK)
        bi[0:1, cols] = jnp.where(lane < 64, a, pltpu.roll(b, 64, 1))
        bi[1:2, cols] = jnp.where(lane < 64, pltpu.roll(a, 64, 1), b)


def qkv_part(normed, w, cosine, sine, q, kv):
    for i in range(HALF // QB):
        rows = slice(i * QB, i * QB + QB)
        out = dot(normed[rows, :], w).astype(bf16).astype(f32)
        cb = cosine[rows, :]
        sb = sine[rows, :]
        kv[rows, :BLK] = turn(out[:, BLK : 2 * BLK], cb, sb).astype(bf16)
        kv[rows, BLK:] = out[:, 2 * BLK :].astype(bf16)
        q[rows, :] = (turn(out[:, :BLK], cb, sb).astype(bf16).astype(f32) * 0.125).astype(bf16)


def take_blocks(ids, blocks, room, sems, at=0):
    part = slice(at, at + BLK)
    return copy_all([(blocks[2 * r + s].at[part], room.at[rows_of(ids, r, s)]) for r in range(4) for s in range(2)], sems)


def qkv_first_kernel(ids, *refs):
    blocks, (wq, cosine, sine), refs = refs[:8], refs[8:11], refs[11:]
    normed, xhat, q, kv, gain, bias, bfc, bi, raw, sems = refs
    copies = take_blocks(ids, blocks, raw, sems)
    w = wq.here()
    params_part([w[f, BLK:, :] for f in range(8)], gain, bias, bfc, bi)
    wait_all(copies)
    for i in range(HALF // QB):
        rows = slice(i * QB, i * QB + QB)
        x, _ = stats(raw[rows, :].astype(f32))
        xhat[rows, :] = x.astype(bf16)
        normed[rows, :] = (x * gain[0:1, :] + bias[0:1, :]).astype(bf16)
    xhat.send()
    normed.send()
    qkv_part(normed, w[:, :BLK, :].reshape(D, 384), cosine, sine, q, kv)


def qkv_kernel(ids, *refs):
    blocks, w, (cosine, sine), (normed, q, kv, wq, sems, wsem) = refs[:8], refs[8:9], refs[9:11], refs[11:]
    copies = copy_all(weight_copies(ids, w, slice(1024, 1408), wq), wsem)
    copies += take_blocks(ids, blocks, normed.ref, sems)
    wait_all(copies)
    normed.send()
    qkv_part(normed, wq[...].reshape(D, 384), cosine, sine, q, kv)


def ff_kernel(layer, ids, normed, bi, *refs):
    w, (active, slope, feed, wi, wf, va, vs, vf, wsems, sems) = refs[:-10], refs[-10:]
    copies = copy_all(weight_copies(ids, w, slice(0, 512), wi), wsems.at[0])
    late = copy_all(weight_copies(ids, w, slice(512, 1024), wf), wsems.at[1])
    normed.here()
    wait_all(copies)
    left = right = None
    sent = []
    for i in range(HALF // QB):
        rows = slice(i * QB, i * QB + QB)
        pre = dot(normed[rows, :], wi[...].reshape(D, 512)) + bi[layer : layer + 1, :]
        act, der = gelu_both(pre)
        act = act.astype(bf16)
        va[rows, :] = act
        vs[rows, :] = der.astype(bf16)
        if i == 0:
            wait_all(late)
            left, right = wf[:, 0:64, :].reshape(512, 512), wf[:, 64:128, :].reshape(512, 512)
        vf[rows, :512] = dot(act, left).astype(bf16)
        vf[rows, 512:] = dot(act, right).astype(bf16)
        pairs = [(v.at[rows], out.at[rows]) for v, out in ((va, active), (vs, slope), (vf, feed))]
        sent += copy_all(pairs, sems.at[i])
    wait_all(sent)


def ff(ids, layer, normed, w, bi):
    room = lambda *shape: pltpu.VMEM(shape, bf16)
    return call(
        functools.partial(ff_kernel, layer), "ff", [((HALF, 512), bf16), ((HALF, 512), bf16), ((HALF, D), bf16)],
        (ids, normed, bi, *w), 5,
        [room(8, BLK, 512), room(8, BLK, 512), room(HALF, 512), room(HALF, 512), room(HALF, D),
         pltpu.SemaphoreType.DMA((2, 4)), pltpu.SemaphoreType.DMA((4, 3))],
        raw=range(3, 3 + len(w)), out_raw=(0, 1, 2), limit=62 - 11 * layer,
    )


def head_cut(x):
    lane = lax.broadcasted_iota(jnp.int32, x.shape, 1)
    zero = jnp.zeros((), x.dtype)
    return [jnp.where(lane < 64, x, zero), jnp.where(lane >= 64, x, zero)]


def seen(i, kk, qseg, kseg):
    q0 = i * QB
    qs = qseg[0:1, q0 : q0 + QB]
    ks = kseg[0:kk, 0:1]
    key = lax.broadcasted_iota(jnp.int32, (kk, QB), 0)
    query = q0 + lax.broadcasted_iota(jnp.int32, (kk, QB), 1)
    return (key <= query) & ((ks == 0) | (ks == qs))


def flip(x):
    return jnp.transpose(x.astype(f32)).astype(bf16)


def attn_own_kernel(ids, q, kv, qseg, acc, m_out, l_out):
    qseg = qseg[...]
    kseg = jnp.transpose(qseg)
    km = head_cut(kv[:, :BLK])
    vt = flip(kv[:, BLK:])
    for i in range(HALF // QB):
        cols = slice(i * QB, (i + 1) * QB)
        kk = (i + 1) * QB
        allowed = seen(i, kk, qseg, kseg)
        for h in range(2):
            rows = slice(h * 64, h * 64 + 64)
            s = jnp.where(allowed, dot_nt(km[h][:kk], q[cols, :]), -1e30)
            m = jnp.max(s, axis=0, keepdims=True)
            p = jnp.exp(s - m)
            l_out[h : h + 1, cols] = jnp.sum(p, axis=0, keepdims=True)
            m_out[h : h + 1, cols] = m
            acc[rows, cols] = dot(vt[rows, :kk], p.astype(bf16))


def split_rows(ids, mine, away, block):
    for r in range(4):
        away[r] = block(rows_of(ids, r, 1)).astype(bf16)
    away.send()
    for r in range(4):
        mine[r] = block(rows_of(ids, r, 0)).astype(bf16)


def attn_full_kernel(ids, q, kv0, acc, m_in, l_in, feed, wo, attn, lse, mine, away, tmp):
    upper = ids[2] == 1
    for ref in (q, kv0, acc, m_in, l_in):
        ref.here()

    @pl.when(upper)
    def _():
        km = head_cut(kv0[:, :BLK])
        vt = flip(kv0[:, BLK:])
        for i in range(HALF // QB):
            cols = slice(i * QB, (i + 1) * QB)
            for h in range(2):
                rows = slice(h * 64, h * 64 + 64)
                s = dot_nt(km[h], q[cols, :])
                m0 = m_in[h : h + 1, cols]
                m = jnp.maximum(m0, jnp.max(s, axis=0, keepdims=True))
                p = jnp.exp(s - m)
                a = jnp.exp(m0 - m)
                l = l_in[h : h + 1, cols] * a + jnp.sum(p, axis=0, keepdims=True)
                o = dot(vt[rows, :], p.astype(bf16))
                tmp[rows, cols] = (acc[rows, cols] * a + o) / l
                lse[h : h + 1, cols] = m + jnp.log(l)

    @pl.when(jnp.logical_not(upper))
    def _():
        for h in range(2):
            rows = slice(h * 64, h * 64 + 64)
            l = l_in[h : h + 1, :]
            tmp[rows, :] = acc[rows, :] / l
            lse[h : h + 1, :] = m_in[h : h + 1, :] + jnp.log(l)

    attn[...] = jnp.transpose(tmp[...]).astype(bf16)
    attn.send()
    lse.send()
    split_rows(ids, mine, away, lambda rows: feed[rows, :].astype(f32) + dot(attn[rows, :], wo[...]))


def mid_kernel(ids, mine, got, total, one, two, three):
    for r, out in ((1, one), (2, two), (3, three)):
        out[...] = (mine[r].astype(f32) + got[r].astype(f32)).astype(bf16)
    total[...] = mine[0].astype(f32) + got[0].astype(f32)


def summed(total, one, two, three):
    return total[...] + one[...].astype(f32) + two[...].astype(f32) + three[...].astype(f32)


def fwd_end_kernel(ids, total, one, two, three, x, gain, bias, bfc, x_new, normed):
    new = x[...].astype(f32) + summed(total, one, two, three) + bfc[0:1, :]
    x_new[...] = new
    xhat, _ = stats(new)
    normed[...] = (xhat * gain[1:2, :] + bias[1:2, :]).astype(bf16)


def last_end_kernel(ids, total, one, two, three, x, bfc, out):
    out[...] = (x[...] + summed(total, one, two, three) + bfc[1:2, :]).astype(bf16)


def grad_in_kernel(at, ids, *refs):
    blocks, (wo, gr, dattn, sems) = refs[:8], refs[8:]
    wait_all(take_blocks(ids, blocks, gr.ref, sems, at))
    gr.send()
    dattn[...] = dot_nt(gr[...], wo[...]).astype(bf16)


def row_delta(attn, do):
    prod = attn[...].astype(f32) * do[...].astype(f32)
    head = lax.broadcasted_iota(jnp.int32, (8, BLK), 0)
    lane = lax.broadcasted_iota(jnp.int32, (8, BLK), 1) // 64
    pickers = jnp.where(head == lane, 1.0, 0.0).astype(f32)
    return lax.dot_general(pickers, prod, NT, precision=lax.Precision.HIGHEST, preferred_element_type=f32)


def grad_block(km, vm, kt, qm, dom, q_blk, do_blk, lse, delta, allowed):
    p = jnp.exp(dot_nt(km, q_blk) - lse)
    if allowed is not None:
        p = jnp.where(allowed, p, 0.0)
    dp = dot_nt(vm, do_blk)
    ds = (p * (dp - delta)).astype(bf16)
    return dot(kt, ds), dot(ds, qm), dot(p.astype(bf16), dom)


def grad_full_kernel(ids, q, kv0, do, attn, lse, dqt, dkv, acck, accv):
    upper = ids[2] == 1
    for ref in (q, kv0, do, attn, lse):
        ref.here()

    @pl.when(upper)
    def _():
        delta = row_delta(attn, do)
        qm, km, vm, dom = [head_cut(x) for x in (q[...], kv0[:, :BLK], kv0[:, BLK:], do[...])]
        kt = flip(kv0[:, :BLK])
        for i in range(HALF // QB):
            cols = slice(i * QB, (i + 1) * QB)
            for h in range(2):
                rows = slice(h * 64, h * 64 + 64)
                dq, dk, dv = grad_block(
                    km[h], vm[h], kt[rows, :], qm[h][cols], dom[h][cols], q[cols, :], do[cols, :],
                    lse[h : h + 1, cols], delta[h : h + 1, cols], None,
                )
                dqt[rows, cols] = dq
                if i == 0 and h == 0:
                    acck[...] = dk
                    accv[...] = dv
                else:
                    acck[...] += dk
                    accv[...] += dv
        dkv[:, :BLK] = acck[...].astype(bf16)
        dkv[:, BLK:] = accv[...].astype(bf16)

    @pl.when(jnp.logical_not(upper))
    def _():
        dqt[...] = jnp.zeros(dqt.shape, f32)
        dkv[...] = jnp.zeros(dkv.shape, bf16)


def grad_own_kernel(ids, q, kv, do, attn, lse, qseg, dqt0, dq_out, dk_out, dv_out, tmp):
    qseg = qseg[...]
    kseg = jnp.transpose(qseg)
    delta = row_delta(attn, do)
    qm, km, vm, dom = [head_cut(x) for x in (q[...], kv[:, :BLK], kv[:, BLK:], do[...])]
    kt = flip(kv[:, :BLK])
    dk_out[...] = jnp.zeros(dk_out.shape, f32)
    dv_out[...] = jnp.zeros(dv_out.shape, f32)
    for i in range(HALF // QB):
        cols = slice(i * QB, (i + 1) * QB)
        kk = (i + 1) * QB
        allowed = seen(i, kk, qseg, kseg)
        for h in range(2):
            rows = slice(h * 64, h * 64 + 64)
            dq, dk, dv = grad_block(
                km[h][:kk], vm[h][:kk], kt[rows, :kk], qm[h][cols], dom[h][cols], q[cols, :], do[cols, :],
                lse[h : h + 1, cols], delta[h : h + 1, cols], allowed,
            )
            tmp[rows, cols] = (dq + dqt0[rows, cols]) * 0.125
            dk_out[:kk, :] += dk
            dv_out[:kk, :] += dv
    dq_out[...] = jnp.transpose(tmp[...])


def ff_back_outer_kernel(ids, gr, slope, active, attn, normed, *refs):
    w, (part, dbi, out, wi, wf, vd, v, wsems, sems) = refs[:-9], refs[-9:]
    copies = copy_all(weight_copies(ids, w, slice(512, 1024), wf), wsems.at[0])
    late = copy_all(weight_copies(ids, w, slice(0, 512), wi), wsems.at[1])
    gr.here()
    slope.here()
    wait_all(copies)
    left, right = wf[:, 0:64, :].reshape(512, 512), wf[:, 64:128, :].reshape(512, 512)
    total = jnp.zeros((1, 512), f32)
    for i in range(HALF // QB):
        rows = slice(i * QB, i * QB + QB)
        d = (dot_nt(gr[rows, :512], left) + dot_nt(gr[rows, 512:], right)) * slope[rows, :].astype(f32)
        total = total + jnp.sum(d, axis=0, keepdims=True)
        d = d.astype(bf16)
        vd[rows, :] = d
        if i == 0:
            wait_all(late)
        part[rows, :] = dot_nt(d, wi[...].reshape(D, 512)).astype(bf16)
    part.send()
    dbi[...] = jnp.concatenate([total, jnp.zeros((7, 512), f32)], 0)
    wait_all(outer_rows(out, v, sems, active, gr, attn, normed, vd))


def ff_back_outer(ids, rows, gr, slope, active, attn, normed, w, after):
    room = lambda *shape: pltpu.VMEM(shape, bf16)
    return call(
        ff_back_outer_kernel, "ff_back_outer", [((HALF, D), bf16), ((8, 512), f32), ((8, rows, 512), bf16)],
        (ids, gr, slope, active, attn, normed, *w), 9,
        [room(8, BLK, 512), room(8, BLK, 512), room(HALF, 512), room(8, 288, 512), pltpu.SemaphoreType.DMA((2, 4)),
         pltpu.SemaphoreType.DMA((3, 2))],
        raw=range(6, 6 + len(w)), out_raw=(2,), after=after,
    )


def combine_rows(ids, dq, dk, dv, back, cosine, sine, dqkv):
    cb = cosine[...]
    sb = -sine[...]
    dqkv[:, :BLK] = turn(dq[...], cb, sb).astype(bf16)
    dqkv[:, BLK : 2 * BLK] = turn(dk[...] + back[:, :BLK].astype(f32), cb, sb).astype(bf16)
    dqkv[:, 2 * BLK :] = (dv[...] + back[:, BLK:].astype(f32)).astype(bf16)


def combine_kernel(ids, dq, dk, dv, back, cosine, sine, part, w1, normed, _, mine, away, payload, dqkv, out, wq, wsem):
    copies = copy_all(weight_copies(ids, (w1,), slice(1024, 1408), wq), wsem)
    combine_rows(ids, dq, dk, dv, back, cosine, sine, dqkv)
    wait_all(copies)
    w = wq[...].reshape(D, 384)
    split_rows(ids, mine, away, lambda rows: part[rows, :].astype(f32) + dot_nt(dqkv[rows, :], w))
    mine.send()
    g_q = outer(normed[...], dqkv[...])
    for f in range(8):
        pack_rows(out, f, g_q)
    wait_all(copy_all([(out, payload.at[:, 288:384])], wsem))


def combine_first_kernel(ids, dq, dk, dv, back, cosine, sine, part, wq0, xhat, normed, sums1, dbi0, dbi1, *refs):
    _, mine, away, payload, dqkv, out, sems = refs
    combine_rows(ids, dq, dk, dv, back, cosine, sine, dqkv)
    w = wq0[:, :BLK, :].reshape(D, 384)
    gain = jnp.zeros((1, D), f32)
    base = jnp.zeros((1, D), f32)
    for s, to in ((1, away), (0, mine)):
        for r in range(4):
            rows = rows_of(ids, r, s)
            block = part[rows, :].astype(f32) + dot_nt(dqkv[rows, :], w)
            to[r] = block.astype(bf16)
            gain = gain + jnp.sum(block * xhat[rows, :].astype(f32), axis=0, keepdims=True)
            base = base + jnp.sum(block, axis=0, keepdims=True)
        to.send()
    g_q = outer(normed[...], dqkv[...])
    lane = lax.broadcasted_iota(jnp.int32, (1, BLK), 1)
    blank = jnp.zeros((13, 384), f32)
    none = jnp.zeros((1, 256), f32)
    for f in range(8):
        pack_rows(out, f, g_q)
        cols = slice(f * BLK, f * BLK + BLK)
        row0 = jnp.concatenate([gain[:, cols], base[:, cols], sums1[3:4, cols]], 1)
        row1 = jnp.concatenate([sums1[0:1, cols], sums1[1:2, cols], sums1[2:3, cols]], 1)
        half = slice((f // 2) * BLK, (f // 2) * BLK + BLK)
        a = dbi0[0:1, half]
        b = dbi1[0:1, half]
        if f % 2 == 0:
            b = pltpu.roll(b, 64, 1)
        else:
            a = pltpu.roll(a, 64, 1)
        row2 = jnp.concatenate([jnp.where(lane < 64, a, b), none], 1)
        out[f, 96:112, :384] = jnp.concatenate([row0, row1, row2, blank], 0).astype(bf16)
        out[f, 96:112, 384:] = jnp.zeros((16, 128), bf16)
    wait_all(copy_all([(out, payload.at[:, 288:400])], sems))


def norm_back(dn, x, gain_row, g):
    xhat, inv = stats(x[...].astype(f32))
    dx = dn * gain_row
    dx = inv * (dx - jnp.mean(dx, -1, keepdims=True) - xhat * jnp.mean(dx * xhat, -1, keepdims=True))
    return xhat, g[...].astype(f32) + dx


def bwd_end_kernel(ids, total, one, two, three, x, gain, g, g_new, gr, sums):
    dn = summed(total, one, two, three)
    xhat, new = norm_back(dn, x, gain[1:2, :], g)
    g_new[...] = new
    gr[...] = new.astype(bf16)
    col = lambda v: jnp.sum(v, axis=0, keepdims=True)
    top = col(g[...].astype(f32))
    sums[...] = jnp.concatenate([col(dn * xhat), col(dn), top, col(new), jnp.zeros((4, D), f32)], 0)


def bwd_last_kernel(ids, total, one, two, three, x, gain, g, g_new):
    _, new = norm_back(summed(total, one, two, three), x, gain[0:1, :], g)
    g_new[...] = new


def outer(a, b):
    return lax.dot_general(a, b, (((0,), (0,)), ((), ())), preferred_element_type=f32).astype(bf16)


def pack_rows(out, f, g_q):
    for part in range(3):
        for group in range(4):
            piece = g_q[f * 128 + group * 32 : f * 128 + group * 32 + 32, part * BLK : part * BLK + BLK]
            out[f, part * 32 : part * 32 + 32, group * BLK : group * BLK + BLK] = piece


def outer_rows(out, v, sems, active, gr, attn, normed, dpre):
    for half in range(2):
        cols = slice(half * 512, half * 512 + 512)
        g_f = outer(active[...], gr[:, cols])
        g_o = outer(attn[...], gr[:, cols])
        for f in range(8):
            v[f, 128 + 64 * half : 192 + 64 * half, :] = g_f[f * 64 : f * 64 + 64]
            v[f, 256 + 16 * half : 272 + 16 * half, :] = g_o[f * 16 : f * 16 + 16]
    first = copy_all([(v.at[:, 128:288], out.at[:, 128:288])], sems.at[0])
    for half in range(2):
        cols = slice(half * 512, half * 512 + 512)
        g_i = outer(normed[:, cols], dpre[...])
        for k in range(4):
            v[4 * half + k, 0:128, :] = g_i[k * 128 : k * 128 + 128]
        group = slice(4 * half, 4 * half + 4)
        first += copy_all([(v.at[group, 0:128], out.at[group, 0:128])], sems.at[1 + half])
    return first


def fsum_kernel(ids, *refs):
    gots, (low, piece) = refs[:-2], refs[-2:]
    at = 0
    for got in gots:
        rows, cols = got.shape[1:]
        for start in range(0, rows, 16):
            part = slice(start, start + 16)
            total = got[0, part, :].astype(f32)
            for f in range(1, 8):
                total = total + got[f, part, :].astype(f32)
            total = total.astype(bf16)
            if 256 <= at < 288:
                piece[at - 256 : at - 240, :] = total
            else:
                to = at if at < 256 else at - 32
                low[to : to + 16, :cols] = total
                if cols < 512:
                    low[to : to + 16, cols:] = jnp.zeros((16, 512 - cols), bf16)
            at += 16


def add_rows(terms, start, stop):
    total = terms[0][start:stop, :].astype(f32)
    for term in terms[1:]:
        total = total + term[start:stop, :].astype(f32)
    return total.astype(bf16)


def xsum_top_kernel(ids, low, got, main):
    main[...] = add_rows((low, got), 0, 352)


def xsum_last_kernel(ids, low, got, p0, p0_other, p1, p1_other, main):
    terms = (low, got)
    main[0:112, :] = add_rows(terms, 256, 368)
    main[112:368, :] = add_rows(terms, 0, 256)
    main[368:400, :] = add_rows((p0, p0_other), 0, 32)
    main[400:432, :] = add_rows((p1, p1_other), 0, 32)


def over_groups(ids, name, gots, after=()):
    rows = sum(got.shape[1] for got in gots)
    low, piece = call(fsum_kernel, name, [((rows - 32, 512), bf16), ((32, 512), bf16)], (ids, *gots), 3, after=after)
    return low, transpose_owner(piece)


def by_core(ids, mine, other):
    return jnp.where(ids[1] == 0, mine, other), jnp.where(ids[1] == 0, other, mine)


def place_in(ids, mine, other, y, at, o_i, o_f):
    lane = lax.broadcasted_iota(jnp.int32, (BLK, BLK), 1)
    for half in range(2):
        rows = slice(at + 128 + 64 * half, at + 192 + 64 * half)
        zero, one = by_core(ids, mine[y, rows, :], other[y, rows, :])
        cols = slice(half * 512, half * 512 + 512)
        o_f[y * BLK : y * BLK + 64, cols] = zero.astype(f32)
        o_f[y * BLK + 64 : y * BLK + BLK, cols] = one.astype(f32)
    for pair in range(4):
        cols = slice(pair * BLK, pair * BLK + BLK)
        a, b = by_core(ids, mine[y, at : at + BLK, cols].astype(f32), other[y, at : at + BLK, cols].astype(f32))
        even = 2 * pair * 512 + y * BLK
        o_i[:, even : even + BLK] = jnp.where(lane < 64, a, pltpu.roll(b, 64, 1))
        odd = even + 512
        o_i[:, odd : odd + BLK] = jnp.where(lane < 64, pltpu.roll(a, 64, 1), b)


def place_q(ids, mine, other, y, at, o_q):
    for part in range(3):
        rows = slice(at + part * 32, at + part * 32 + 32)
        start = part * D + 2 * y * BLK
        for group in range(4):
            cols = slice(group * BLK, group * BLK + BLK)
            zero, one = by_core(ids, mine[y, rows, cols], other[y, rows, cols])
            to = slice(group * 32, group * 32 + 32)
            o_q[to, start : start + BLK] = zero.astype(f32)
            o_q[to, start + BLK : start + 2 * BLK] = one.astype(f32)


def fetch_rows(ids, blocks, room_a, room_b, sems):
    pairs = []
    for r in range(4):
        y = lax.rem(ids[0] + r, 4)
        pairs += [(blocks[2 * r], room_a.at[y]), (blocks[2 * r + 1], room_b.at[y])]
    wait_all(copy_all(pairs, sems))


def assemble_top_kernel(ids, *refs):
    blocks, (o_i, o_f, o_q, vi, vf, vq, ra, rb, sems, out_sems) = refs[:8], refs[8:]
    fetch_rows(ids, blocks, ra, rb, sems)
    for y in range(4):
        place_in(ids, ra, rb, y, 0, vi, vf)
        place_q(ids, ra, rb, y, 256, vq)
    outs = copy_all([(vi, o_i.at[1]), (vf, o_f.at[1]), (vq, o_q.at[1])], out_sems)
    wait_all(outs)


def finish_kernel(ids, *refs):
    blocks, refs = refs[:8], refs[11:]
    o_i, o_f, o_q, o_o, o_g, o_s, o_bf, o_bi, vi, vf, vq, ra, rb, sems, out_sems = refs
    fetch_rows(ids, blocks, ra, rb, sems)
    total = jnp.zeros((16, 384), f32)
    lane = lax.broadcasted_iota(jnp.int32, (1, BLK), 1)
    for y in range(4):
        place_q(ids, ra, rb, y, 0, vq)
        place_in(ids, ra, rb, y, 112, vi, vf)
    outs = copy_all([(vi, o_i.at[0]), (vf, o_f.at[0]), (vq, o_q.at[0])], out_sems)
    for y in range(4):
        for layer in range(2):
            for half in range(2):
                at = 368 + 32 * layer + 16 * half
                zero, one = by_core(ids, ra[y, at : at + 16, :], rb[y, at : at + 16, :])
                cols = slice(half * 512, half * 512 + 512)
                o_o[layer, 32 * y : 32 * y + 16, cols] = zero.astype(f32)
                o_o[layer, 32 * y + 16 : 32 * y + 32, cols] = one.astype(f32)
        zero, one = by_core(ids, ra[y, 96:112, :384].astype(f32), rb[y, 96:112, :384].astype(f32))
        total = total + zero + one
        a, b = zero[2:3, :BLK], one[2:3, :BLK]
        cols = slice(y * BLK, y * BLK + BLK)
        o_bi[0:1, cols] = jnp.where(lane < 64, a, pltpu.roll(b, 64, 1))
        o_bi[1:2, cols] = jnp.where(lane < 64, pltpu.roll(a, 64, 1), b)
    o_g[...] = total[0:2, :BLK]
    o_s[...] = total[0:2, BLK : 2 * BLK]
    o_bf[...] = total[0:2, 2 * BLK :]
    wait_all(outs)


def positions_of(group_seg):
    token_index = jnp.arange(group_seg.shape[0], dtype=jnp.int32)
    labels = jnp.arange(CONTS + 1, dtype=jnp.int32)
    member = (group_seg[:, None] == labels[None, :]).astype(jnp.int32)
    counts = jnp.sum(member, axis=0)
    starts = jnp.cumsum(counts) - counts
    own_start = jnp.sum(member * starts[None, :], axis=1)
    return token_index - own_start + jnp.where(group_seg > 0, counts[0], 0)


def rope_tables(positions):
    lane = jnp.arange(BLK, dtype=jnp.int32) % 64
    inverse = 10000.0 ** (-2.0 * (lane // 2).astype(f32) / ROT)
    phase = positions.astype(f32)[:, None] * jnp.where(lane < ROT, inverse, 0.0)[None, :]
    sign = jnp.where(lane % 2 == 0, -1.0, 1.0)
    return jnp.cos(phase), jnp.sin(phase) * sign[None, :]


def scatter(ids, mine, away):
    got = shift(away, "core", 1, 2)
    blk = (BLK, D)
    total, one, two, three = call(
        mid_kernel, "rs_mid", [(blk, f32)] + [(blk, bf16)] * 3, (ids, mine, got), 2, vm=(2,), out_vm=(0, 1, 2, 3), limit=8
    )
    return [total] + spread([one, two, three]), one


def grad_in(ids, g_blocks, wo, at):
    return call(
        functools.partial(grad_in_kernel, at), "grad_in", [((HALF, D), bf16), ((HALF, BLK), bf16)], (ids, *g_blocks, wo), 3,
        [dma(8)], raw=range(1, 9),
    )


def body(tokens, segment, ln_gain, ln_bias, w_qkv, w_out, w_in, b_in, w_fc, b_fc, cotangent):
    xh = lax.axis_index("xh")
    ids = jnp.stack([lax.axis_index("y"), lax.axis_index("core"), xh, lax.axis_index("xl"), lax.axis_index("z")]).astype(jnp.int32)
    own = tokens[0]
    full = (HALF, D)
    blk = (BLK, D)
    head = (HALF, BLK)
    room = lambda shape, kind=f32: pltpu.VMEM(shape, kind)
    chunks = [room((8, BLK, BLK), bf16)]

    group_seg = segment[0]
    positions = positions_of(group_seg)
    seg = lax.dynamic_slice_in_dim(group_seg, xh * HALF, HALF, 0)
    cosine, sine = rope_tables(lax.dynamic_slice_in_dim(positions, xh * HALF, HALF, 0))
    qseg = jnp.broadcast_to(seg[None, :].astype(f32), (8, HALF))

    (both,) = call(
        join_kernel, "join", [((2 * BLK, D), bf16)], (ids, own, cotangent[0]), 1, [dma(2)], raw=(1, 2), limit=62
    )
    (p0,) = call(
        pack_first_kernel, "pack_first", [(blk, bf16)], (ids, w_in, w_fc), 3, chunks + [dma(10)], raw=(1, 2), limit=62, after=(both,),
    )
    other0 = shift(p0, "xl", 1, 2)
    (q0,) = call(
        pack_q_kernel, "pack_q", [((8, 144, 384), bf16)], (ids, w_qkv, ln_gain, ln_bias, b_fc, b_in), 3,
        [room((144, 384), bf16), room((3, 2, BLK), bf16), room((2, 512), bf16), dma(7), dma(8)],
        raw=(1, 2, 3, 4, 5), out_raw=(0,), after=(cosine, other0), limit=62,
    )
    wq0 = lax.all_to_all(q0, FS, 0, 0, tiled=True)
    (p1,) = call(
        pack_second_kernel, "pack_second", [((BLK, 1408), bf16)], (ids, w_in, w_fc, w_qkv), 3, chunks + [dma(13)], raw=(1, 2, 3), limit=62,
        after=(wq0,),
    )
    tok_blocks = gather_blocks(both, lambda *x: gate_all(ids, x, (q0,)))
    w0 = gather_fsdp(ids, p0, other0)

    def attend_own(layer, q, kv, normed, w):
        kv0 = lax.ppermute(kv, "xh", [(0, 1)])
        act = ff(ids, layer, normed, w, bi)
        own_part = call(
            attn_own_kernel, "attn_own", [((BLK, HALF), f32), ((2, HALF), f32), ((2, HALF), f32)], (ids, q, kv, qseg), 5
        )
        return kv0, act, own_part

    def attend_full(layer, q, kv0, act, own_part, after):
        active, slope, feed = act
        attn, lse, mine, away = call(
            attn_full_kernel, "attn_full", [(head, bf16), ((2, HALF), f32)] + [((4, BLK, D), bf16)] * 2,
            (ids, q, kv0, *own_part, feed, wo[layer]), 8, [room((BLK, HALF))], after=after,
        )
        return (kv0, active, slope, attn, lse), (mine, away)

    normed0, xhat0, q_0, kv_0, gain, bias, bfc, bi = call(
        qkv_first_kernel, "qkv_first",
        [(full, bf16), (full, bf16), (head, bf16), ((HALF, 256), bf16)] + [((2, D), f32)] * 3 + [((2, 512), f32)],
        (ids, *tok_blocks, wq0, cosine, sine), 6, [room(full, bf16), dma(8)], raw=range(1, 9), out_vm=(4, 5, 6, 7),
        limit=62,
    )

    def fetch_wo(layer, after):
        (out,) = call(
            functools.partial(pass_kernel, layer), "pass_wo", [(blk, bf16)], (ids, w_out), 1, [dma(1)], raw=(1,), after=after,
            limit=62,
        )
        return transpose_owner(out)

    wo = [fetch_wo(0, (q_0,))]
    kv0, act, own_part = attend_own(0, q_0, kv_0, normed0, w0)
    (four,) = call(
        four_kernel, "four", [((4, 2, BLK, 1408), bf16)], (ids, p1, shift(p1, "xl", 1, 2)), 2, [dma(8)], out_raw=(0,),
        after=(own_part[1],), limit=62,
    )
    saved0, ends = attend_full(0, q_0, kv0, act, own_part, ())
    w1 = [lax.all_to_all(gate(ids, four, (saved0[3],)), "z", 0, 0, tiled=True).reshape(8, BLK, 1408)]
    terms, sent = scatter(ids, *ends)
    x1, normed_own = call(
        fwd_end_kernel, "fwd_end", [(blk, f32), (blk, bf16)], (ids, *terms, own, gain, bias, bfc), 2,
        vm=range(1, 9), out_vm=(0, 1), limit=8,
    )
    blocks = gather_blocks(normed_own)
    normed1, q_1, kv_1 = call(
        qkv_kernel, "qkv", [(full, bf16), (head, bf16), ((HALF, 256), bf16)], (ids, *blocks, *w1, cosine, sine), 4,
        [room((8, BLK, 384), bf16), dma(8), dma(1)], raw=range(1, 10),
    )
    kv0, act, own_part = attend_own(1, q_1, kv_1, normed1, w1)
    wo.append(fetch_wo(1, (q_1,)))
    gr_top, dattn_top = grad_in(ids, tok_blocks, wo[1], BLK)
    saved1, ends = attend_full(1, q_1, kv0, act, own_part, ())
    terms, _ = scatter(ids, *ends)
    (mixed,) = call(
        last_end_kernel, "last_end", [(blk, bf16)], (ids, *terms, x1, bfc), 2, vm=range(1, 7), out_vm=(0,), limit=8
    )

    def back(q, kv, normed, w, saved, gr, dattn, rows):
        kv0, active, slope, attn, lse = saved
        dqt0, dkv0 = call(
            grad_full_kernel, "grad_full", [((BLK, HALF), f32), ((HALF, 256), bf16)], (ids, q, kv0, dattn, attn, lse), 8,
            [room(head)] * 2,
        )
        got = lax.ppermute(dkv0, "xh", [(1, 0)])
        part, dbi, payload = ff_back_outer(ids, rows, gr, slope, active, attn, normed, w, (dqt0,))
        pieces = call(
            grad_own_kernel, "grad_own", [(head, f32)] * 3, (ids, q, kv, dattn, attn, lse, qseg, dqt0), 5, [room((BLK, HALF))]
        )
        return pieces, got, payload, part, dbi

    part_outs = [((4, BLK, D), bf16), ((4, BLK, D), bf16)]
    pieces, got, payload1, part, dbi1 = back(q_1, kv_1, normed1, w1, saved1, gr_top, dattn_top, 384)
    mine, away, payload1 = call(
        combine_kernel, "combine", part_outs + [((8, 384, 512), bf16)],
        (ids, *pieces, got, cosine, sine, part, *w1, normed1, payload1), 6,
        [room((HALF, 384), bf16), room((8, 96, 512), bf16), room((8, BLK, 384), bf16), dma(1)], raw=(8, 10), out_raw=(2,),
        alias={10: 2}, after=(mixed,),
    )
    terms, sent = scatter(ids, mine, away)
    got_a = lax.all_to_all(payload1, FS, 0, 0, tiled=True)
    g1, gr1, sums1 = call(
        bwd_end_kernel, "bwd_end", [(blk, f32), (blk, bf16), ((8, D), f32)], (ids, *terms, x1, gain, cotangent[0]), 2,
        vm=range(1, 8), out_vm=(0, 1, 2), limit=8,
    )
    g_blocks = gather_blocks(gr1)
    gr, dattn = grad_in(ids, g_blocks, wo[0], 0)
    pieces, got, payload, part, dbi0 = back(q_0, kv_0, normed0, w0, saved0, gr, dattn, 400)
    low1, p1 = over_groups(ids, "fsum_top", (got_a,), pieces[:1])
    (main1,) = call(xsum_top_kernel, "xsum_top", [((352, 512), bf16)], (ids, low1, shift(low1, "xh", 1, 2)), 2)
    mine, away, payload = call(
        combine_first_kernel, "combine_first", part_outs + [((8, 400, 512), bf16)],
        (ids, *pieces, got, cosine, sine, part, wq0, xhat0, normed0, sums1, dbi0, dbi1, payload), 9,
        [room((HALF, 384), bf16), room((8, 112, 512), bf16), dma(1)], raw=(14,), out_raw=(2,), alias={14: 2}, after=(main1,),
    )
    terms, sent = scatter(ids, mine, away)
    (g0,) = call(
        bwd_last_kernel, "bwd_last", [(blk, f32)], (ids, *terms, own, gain, g1), 2, vm=range(1, 8), out_vm=(0,), limit=8
    )
    top_rows = gather_blocks(main1)
    shapes = [((2, BLK, 4096), f32), ((2, 512, D), f32), ((2, BLK, 3 * D), f32)]
    rooms = lambda n: [room(s[0][1:]) for s in shapes] + [room((4, n, 512), bf16)] * 2 + [dma(8), dma(3)]
    outs = call(assemble_top_kernel, "assemble_top", shapes, (ids, *top_rows), 5, rooms(352), raw=range(1, 9), out_raw=(0, 1, 2))
    low0, p0 = over_groups(ids, "fsum_first", (lax.all_to_all(payload, FS, 0, 0, tiled=True),), (g0, outs[2]))
    swap = lambda x: shift(x, "xh", 1, 2)
    (last,) = call(
        xsum_last_kernel, "xsum_last", [((432, 512), bf16)], (ids, low0, swap(low0), p0, swap(p0), p1, swap(p1)), 2,
    )
    last_blocks = gather_blocks(last)
    o_i, o_f, o_q, o_o, o_g, o_s, o_bf, o_bi = call(
        finish_kernel, "finish", shapes + [((2, BLK, D), f32)] + [((2, BLK), f32)] * 3 + [((2, 512), f32)],
        (ids, *last_blocks, *outs), 6, rooms(432), raw=range(1, 12), out_raw=(0, 1, 2),
        alias={9: 0, 10: 1, 11: 2},
    )
    return mixed[None], g0[None], o_g, o_s, o_q, o_o, o_i, o_bi, o_f, o_bf


def solution(mesh):
    fine = Mesh(mesh.devices.reshape(2, 4, 2, 4, 2), AXES)
    seq = ("xh", "y", "core")
    tok = P(FS, seq, None)
    two = P(None, FS)
    three = P(None, FS, None)
    in_specs = (tok, P(FS, None), two, two, three, three, three, two, three, two, tok)
    out_specs = (tok, tok, two, two, three, three, three, two, three, two)
    return jax.shard_map(body, mesh=fine, in_specs=in_specs, out_specs=out_specs, check_vma=False)
```

time: 675 us -> 442 us (0.65)
  Pallas kernels: 18 us -> 156 us
  waiting for transfers between devices: 245 us -> 112 us
  local copies, waits for them, and re-layouts: 135 us -> 17.4 us
  other arithmetic: 78.7 us -> 3.58 us
  matrix products: 71.5 us -> 0 us
  starting transfers between devices: 115 us -> 143 us
    pallas_call x8 -> x42, Pallas kernels: 18 us -> 156 us  [call(): pl.pallas_call(run, out_shape=sds(*outs), in_specs=[SM] + [VM if i in vm...]
    dot_general x32 -> x0, matrix products: 71.5 us -> none  [the longest x8 19.7 us: rope(): partner = jnp.dot(v, swap, precision=precision, preferred_element_type=f32)]
    ppermute x4, waiting for transfers between devices: 58.8 us -> 0.01 us  [the longest x2 0.01 us: attend_own(): kv0 = lax.ppermute(kv, 'xh', [(0, 1)])]
    ppermute x42 -> x60, waiting for transfers between devices: 165 us -> 107 us  [shift(): return lax.ppermute(x, axis, [(i, (i + by) % size) for i in range(size)])]
    ppermute x42 -> x60, starting transfers between devices: 51.2 us -> 94 us  [shift(): return lax.ppermute(x, axis, [(i, (i + by) % size) for i in range(size)])]
    slice x37 -> x0, local copies, waits for them, and re-layouts: 42.7 us -> none  [the longest x4 11.8 us: reduce_layer(): o_f = main[:, :, 896:1408].reshape(512, D)]
    another operation x19 -> x1, other arithmetic: 25.8 us -> 0.18 us  [the longest x8 10.4 us: body(): jnp.stack([a, b])]
    reshape x22 -> x0, local copies, waits for them, and re-layouts: 19.1 us -> none  [the longest x2 6.72 us: reduce_layer(): lax.dynamic_slice_in_dim(twice, (4 - y) % 4, 4, 0).reshape(8, ROWS, 1536)]
  transfers between devices with their start and end apart: 54 -> 72, of which waited for: 36 -> 26; matrix products, arithmetic and copies ran while one was open for 27% -> 1% of each run, Pallas kernels for 3% -> 26%
where the time goes in v2:
time: 442 us; the launch traced here: 434 us
  Pallas kernels  156 us (35%)
  starting transfers between devices  143 us (32%)
  waiting for transfers between devices  112 us (25%)
  local copies, waits for them, and re-layouts  17.4 us (4%)
    pallas_call x42, Pallas kernels, call(): pl.pallas_call(run, out_shape=sds(*outs), in_specs=[SM] + [VM if i in vm...  156 us
    ppermute x60, waiting for transfers between devices, shift(): return lax.ppermute(x, axis, [(i, (i + by) % size) for i in range(size)])  107 us
    ppermute x60, starting transfers between devices, shift(): return lax.ppermute(x, axis, [(i, (i + by) % size) for i in range(size)])  94 us
    unnamed x110, local copies, waits for them, and re-layouts  16.8 us
    ppermute x2, starting transfers between devices, attend_own(): kv0 = lax.ppermute(kv, 'xh', [(0, 1)])  13.9 us
    ppermute x4, starting transfers between devices, transpose_owner(): return lax.ppermute(x, ('y', 'core', 'z', 'xl'), pairs)  12.5 us
  transfers between devices with their start and end apart: 72, of which 26 were waited for; matrix products, arithmetic and copies ran while one was open for 1% of the time, Pallas kernels for 26%

profile of v2, /device:TPU:1, one launch (start us, length us, event | category | flops | bytes accessed | tf_op | source)
XLA Modules:
  0.0 433.9 jit_solution(12279793058482907106)
XLA Ops:
  21.3 6.0 %all-to-all-start = ((bf16[8,144,384]{2,1,0:T(8,128)(2,1)}), bf16[8,144,384]{2,1,0:T(8,128)(2,1)}, u32[]{:S(2)}, u32[]{:S(2)}) async-start(bf16[8,144,384]{2,1,0:T(8,128)(2,1)} %pack_q.1.refs_4_), calls=%async_computation | async-start | bytes 1769472 | tf_op jit(solution)/shard_map/all_to_all | solution.py:916
  44.4 7.3 %qkv_first.1 = (bf16[1024,1024]{1,0:T(8,128)(2,1)}, bf16[1024,1024]{1,0:T(8,128)(2,1)}, bf16[1024,128]{1,0:T(8,128)(2,1)}, bf16[1024,256]{1,0:T(8,128)(2,1)}, f3...) custom-call(s32[5]{0:T(128)} %stack.23.refs_0_, ...), custom_call_target="tpu_custom_call" | custom-call | flops 6000000 | bytes 6000 | tf_op jit(solution)/shard_map/qkv_first/pallas_call | solution.py:108
  77.0 7.8 %ff.2 = (bf16[1024,512]{1,0:T(8,128)(2,1)}, bf16[1024,512]{1,0:T(8,128)(2,1)}, bf16[1024,1024]{1,0:T(8,128)(2,1)}) custom-call(s32[5]{0:T(128)} %stack.23.refs_0_, bf16[1024,1024]{1,0:T(8,128)(2,1)} %get-tuple-element.114.refs_1_.refs_5_.refs_10_, f32[2,512]{1,0:T(2,128)} %get-tuple-element.115.refs_2_, bf16[2,128,1024]{2,1,0:T(8,128)(2,1)} %pair.1.refs_3_.refs_6_, ...), custom_call_target="tpu_custom_call" | custom-call | flops 5000000 | bytes 5000 | tf_op jit(solution)/shard_map/ff/pallas_call | solution.py:108
  102.1 6.7 %collective-permute-start.15 = (bf16[128,1024]{1,0:T(8,128)(2,1)S(1)}, bf16[128,1024]{1,0:T(8,128)(2,1)S(1)}, u32[]{:S(2)}, u32[]{:S(2)}) collective-permute-start(bf16[128,1024]{1,0:T(8,128)(2,1)S(1)} %get-tuple-element.121), channel_id=1, source_target_pairs={{0,32},{16,48},{32,0},{48,16},{1,33},{17,49},{33,1},{49,17},{2,34}... | collective-permute-start | bytes 786440 | tf_op jit(solution)/shard_map/ppermute | solution.py:138
  108.8 5.5 %collective-permute-done.14.refs_2_ = bf16[128,1024]{1,0:T(8,128)(2,1)S(1)} collective-permute-done((bf16[128,1024]{1,0:T(8,128)(2,1)S(1)}, bf16[128,1024]{1,0:T(8,128)(2,1)S(1)}, u32[]{:S(2)}, u32[]{:S(2)}) %collective-permute-start.14) | collective-permute-done | bytes 262176 | tf_op jit(solution)/shard_map/ppermute | solution.py:138
  114.3 6.6 %collective-permute-done.15.refs_3_ = bf16[128,1024]{1,0:T(8,128)(2,1)S(1)} collective-permute-done((bf16[128,1024]{1,0:T(8,128)(2,1)S(1)}, bf16[128,1024]{1,0:T(8,128)(2,1)S(1)}, u32[]{:S(2)}, u32[]{:S(2)}) %collective-permute-start.15) | collective-permute-done | bytes 262176 | tf_op jit(solution)/shard_map/ppermute | solution.py:138
  130.7 5.7 %collective-permute-start.19 = (bf16[128,1024]{1,0:T(8,128)(2,1)S(1)}, bf16[128,1024]{1,0:T(8,128)(2,1)S(1)}, u32[]{:S(2)}, u32[]{:S(2)}) collective-permute-start(bf16[128,1024]{1,0:T(8,128)(2,1)S(1)} %collective-permute-done.18.refs_3_), channel_id=1, source_target_pairs={{0,8},{8,0},{1,9},{9,1},{2,10},{10,2},{3,11},{11,3},{4,12},{12,4},... | collective-permute-start | bytes 786440 | tf_op jit(solution)/shard_map/ppermute | solution.py:138
  147.8 9.1 %collective-permute-start.25 = (bf16[1024,256]{1,0:T(8,128)(2,1)}, bf16[1024,256]{1,0:T(8,128)(2,1)S(1)}, u32[]{:S(2)}, u32[]{:S(2)}) collective-permute-start(bf16[1024,256]{1,0:T(8,128)(2,1)} %get-tuple-element.129.refs_2_), channel_id=1, source_target_pairs={{0,64},{1,65},{2,66},{3,67},{4,68},{5,69},{6,70},{7,71},{8,72},{9,... | collective-permute-start | bytes 1572872 | tf_op jit(solution)/shard_map/ppermute | solution.py:925
  162.3 6.2 %attn_own.3 = (f32[128,1024]{1,0:T(8,128)S(1)}, f32[2,1024]{1,0:T(2,128)S(1)}, f32[2,1024]{1,0:T(2,128)S(1)}) custom-call(s32[5]{0:T(128)S(1)} %copy-done.34, bf16[1024,128]{1,0:T(8,128)(2,1)S(1)} %copy-done.6, bf16[1024,256]{1,0:T(8,128)(2,1)} %get-tuple-element.129.refs_2_, f32[8,1024]{1,0:T(8,128)S(1)} %broadcast_in_dim.42.refs_3_.refs_6_), custom_call_target="tpu_custom_call" | custom-call | flops 5000000 | bytes 5000 | tf_op jit(solution)/shard_map/attn_own/pallas_call | solution.py:108
  168.5 8.0 %ff.3 = (bf16[1024,512]{1,0:T(8,128)(2,1)S(1)}, bf16[1024,512]{1,0:T(8,128)(2,1)S(1)}, bf16[1024,1024]{1,0:T(8,128)(2,1)}) custom-call(s32[5]{0:T(128)S(1)} %copy-done.34, bf16[1024,1024]{1,0:T(8,128)(2,1)} %get-tuple-element.133.refs_1_.refs_5_.refs_9_, f32[2,512]{1,0:T(2,128)S(1)} %copy-done.49, bf16[8,128,1408]{2,1,0:T(8,128)(2,1)} %bitcast.12.refs_9_.refs_3_.refs_6_.refs_8_), custom_call_target="tpu_custom_call" | custom-call | flops 5000000 | bytes 5000 | tf_op jit(solution)/shard_map/ff/pallas_call | solution.py:108
  198.5 6.3 %grad_own.2 = (f32[1024,128]{1,0:T(8,128)S(1)}, f32[1024,128]{1,0:T(8,128)S(1)}, f32[1024,128]{1,0:T(8,128)S(1)}) custom-call(s32[5]{0:T(128)S(1)} %copy-done.34, bf16[1024,128]{1,0:T(8,128)(2,1)S(1)} %copy-done.7, bf16[1024,256]{1,0:T(8,128)(2,1)} %get-tuple-element.129.refs_2_, bf16[1024,128]{1,0:T(8,128)(2,1)S(1)} %get-tuple-element.142.refs_3_, ...), custom_call_target="tpu_custom_call" | custom-call | flops 5000000 | bytes 5000 | tf_op jit(solution)/shard_map/grad_own/pallas_call | solution.py:108
  204.8 9.8 %ff_back_outer.2 = (bf16[1024,1024]{1,0:T(8,128)(2,1)}, f32[8,512]{1,0:T(8,128)S(1)}, bf16[8,384,512]{2,1,0:T(8,128)(2,1)}) custom-call(s32[5]{0:T(128)S(1)} %copy-done.34, bf16[1024,1024]{1,0:T(8,128)(2,1)} %get-tuple-element.150.refs_1_, bf16[1024,512]{1,0:T(8,128)(2,1)S(1)} %get-tuple-element.151.refs_2_, ...), custom_call_target="tpu_custom_call" | custom-call | flops 9000000 | bytes 9000 | tf_op jit(solution)/shard_map/ff_back_outer/pallas_call | solution.py:108
  217.0 7.9 %combine.1 = (bf16[4,128,1024]{2,1,0:T(8,128)(2,1)}, bf16[4,128,1024]{2,1,0:T(8,128)(2,1)}, bf16[8,384,512]{2,1,0:T(8,128)(2,1)}) custom-call(s32[5]{0:T(128)S(1)} %copy-done.34, f32[1024,128]{1,0:T(8,128)S(1)} %get-tuple-element.146.refs_1_, f32[1024,128]{1,0:T(8,128)S(1)} %get-tuple-element.147.refs_2_, ...), custom_call_target="tpu_custom_call", output_to_operand_aliasing={{2}: (10, {})} | custom-call | flops 6000000 | bytes 6000 | tf_op jit(solution)/shard_map/combine/pallas_call | solution.py:108
  238.0 11.6 %collective-permute-done.33.refs_2_ = bf16[128,1024]{1,0:T(8,128)(2,1)S(1)} collective-permute-done((bf16[128,1024]{1,0:T(8,128)(2,1)S(1)}, bf16[128,1024]{1,0:T(8,128)(2,1)S(1)}, u32[]{:S(2)}, u32[]{:S(2)}) %collective-permute-start.33) | collective-permute-done | bytes 262176 | tf_op jit(solution)/shard_map/ppermute | solution.py:138
  256.7 9.0 %collective-permute-done.37.refs_3_ = bf16[128,1024]{1,0:T(8,128)(2,1)S(1)} collective-permute-done((bf16[128,1024]{1,0:T(8,128)(2,1)S(1)}, bf16[128,1024]{1,0:T(8,128)(2,1)S(1)}, u32[]{:S(2)}, u32[]{:S(2)}) %collective-permute-start.37) | collective-permute-done | bytes 262176 | tf_op jit(solution)/shard_map/ppermute | solution.py:138
  278.0 6.2 %grad_own.3 = (f32[1024,128]{1,0:T(8,128)S(1)}, f32[1024,128]{1,0:T(8,128)S(1)}, f32[1024,128]{1,0:T(8,128)S(1)}) custom-call(s32[5]{0:T(128)S(1)} %copy-done.34, bf16[1024,128]{1,0:T(8,128)(2,1)S(1)} %copy-done.4, bf16[1024,256]{1,0:T(8,128)(2,1)S(1)} %copy-done.23, bf16[1024,128]{1,0:T(8,128)(2,1)S(1)} %get-tuple-element.162.refs_3_, ...), custom_call_target="tpu_custom_call" | custom-call | flops 5000000 | bytes 5000 | tf_op jit(solution)/shard_map/grad_own/pallas_call | solution.py:108
  288.9 16.9 %collective-permute-start.44 = (bf16[352,512]{1,0:T(8,128)(2,1)S(1)}, bf16[352,512]{1,0:T(8,128)(2,1)S(1)}, u32[]{:S(2)}, u32[]{:S(2)}) collective-permute-start(bf16[352,512]{1,0:T(8,128)(2,1)S(1)} %get-tuple-element.179.refs_1_), channel_id=1, source_target_pairs={{0,64},{64,0},{1,65},{65,1},{2,66},{66,2},{3,67},{67,3},{4,68},{68... | collective-permute-start | bytes 1081352 | tf_op jit(solution)/shard_map/ppermute | solution.py:138
  305.9 10.4 %ff_back_outer.3 = (bf16[1024,1024]{1,0:T(8,128)(2,1)}, f32[8,512]{1,0:T(8,128)S(1)}, bf16[8,400,512]{2,1,0:T(8,128)(2,1)}) custom-call(s32[5]{0:T(128)S(1)} %copy-done.34, bf16[1024,1024]{1,0:T(8,128)(2,1)} %get-tuple-element.169.refs_1_, bf16[1024,512]{1,0:T(8,128)(2,1)} %get-tuple-element.170.refs_2_, bf16[1024,512]{1,0:T(8,128)(2,1)} %get-tuple-element.171.refs_3_, ...), custom_call_target="tpu_custom_call" | custom-call | flops 9000000 | bytes 9000 | tf_op jit(solution)/shard_map/ff_back_outer/pallas_call | solution.py:108
  317.4 7.9 %combine_first.1 = (bf16[4,128,1024]{2,1,0:T(8,128)(2,1)}, bf16[4,128,1024]{2,1,0:T(8,128)(2,1)}, bf16[8,400,512]{2,1,0:T(8,128)(2,1)}) custom-call(s32[5]{0:T(128)S(1)} %copy-done.34, f32[1024,128]{1,0:T(8,128)S(1)} %get-tuple-element.165.refs_2_.refs_1_, f32[1024,128]{1,0:T(8,128)S(1)} %copy-done.36, ...), custom_call_target="tpu_custom_call", output_to_operand_aliasing={{2}: (14, {})} | custom-call | flops 9000000 | bytes 9000 | tf_op jit(solution)/shard_map/combine_first/pallas_call | solution.py:108
  333.3 8.0 %collective-permute-done.50.refs_3_ = bf16[352,512]{1,0:T(8,128)(2,1)S(1)} collective-permute-done((bf16[352,512]{1,0:T(8,128)(2,1)S(1)}, bf16[352,512]{1,0:T(8,128)(2,1)S(1)}, u32[]{:S(2)}, u32[]{:S(2)}) %collective-permute-start.50) | collective-permute-done | bytes 360480 | tf_op jit(solution)/shard_map/ppermute | solution.py:138
  345.1 6.5 %collective-permute-done.54.refs_7_ = bf16[352,512]{1,0:T(8,128)(2,1)S(1)} collective-permute-done((bf16[352,512]{1,0:T(8,128)(2,1)S(1)}, bf16[352,512]{1,0:T(8,128)(2,1)S(1)}, u32[]{:S(2)}, u32[]{:S(2)}) %collective-permute-start.54) | collective-permute-done | bytes 360480 | tf_op jit(solution)/shard_map/ppermute | solution.py:138
  360.7 6.9 %collective-permute-done.46.refs_2_ = bf16[128,1024]{1,0:T(8,128)(2,1)S(1)} collective-permute-done((bf16[128,1024]{1,0:T(8,128)(2,1)S(1)}, bf16[128,1024]{1,0:T(8,128)(2,1)S(1)}, u32[]{:S(2)}, u32[]{:S(2)}) %collective-permute-start.46) | collective-permute-done | bytes 262176 | tf_op jit(solution)/shard_map/ppermute | solution.py:138
  403.8 15.0 %collective-permute-done.62.refs_3_ = bf16[432,512]{1,0:T(8,128)(2,1)S(1)} collective-permute-done((bf16[432,512]{1,0:T(8,128)(2,1)S(1)}, bf16[432,512]{1,0:T(8,128)(2,1)S(1)}, u32[]{:S(2)}, u32[]{:S(2)}) %collective-permute-start.62) | collective-permute-done | bytes 442400 | tf_op jit(solution)/shard_map/ppermute | solution.py:138
  426.2 7.5 %finish.1 = (f32[2,128,4096]{2,1,0:T(8,128)}, f32[2,512,1024]{2,1,0:T(8,128)}, f32[2,128,3072]{2,1,0:T(8,128)}, f32[2,128,1024]{2,1,0:T(8,128)}, f32[2,128]{1,0:...) custom-call(s32[5]{0:T(128)S(1)} %copy-done.34, ...), custom_call_target="tpu_custom_call", output_to_operand_aliasing={{0}: (9, {}), {1}: (10, {}), {2}: (11, {})} | custom-call | flops 6000000 | bytes 6000 | tf_op jit(solution)/shard_map/finish/pallas_call | solution.py:108
  (282 shorter events, 233.4 us)
Async XLA Ops:
  4.0 26.0 %collective-permute-start.1 = (bf16[256,1024]{1,0:T(8,128)(2,1)}, bf16[256,1024]{1,0:T(8,128)(2,1)S(1)}, u32[]{:S(2)}, u32[]{:S(2)}) collective-permute-start(bf16[256,1024]{1,0:T(8,128)(2,1)} %join.1.refs_3_.refs_1_), channel_id=1, source_target_pairs={{0,48},{16,0},{32,16},{48,32},{1,49},{17,1},{33,17},{49,33},{2,50}... | collective-permute-start | bytes 1572872 | tf_op jit(solution)/shard_map/ppermute | solution.py:138
  7.6 22.4 %collective-permute-start.2 = (bf16[256,1024]{1,0:T(8,128)(2,1)}, bf16[256,1024]{1,0:T(8,128)(2,1)S(1)}, u32[]{:S(2)}, u32[]{:S(2)}) collective-permute-start(bf16[256,1024]{1,0:T(8,128)(2,1)} %join.1.refs_3_.refs_1_), channel_id=1, source_target_pairs={{0,32},{16,48},{32,0},{48,16},{1,33},{17,49},{33,1},{49,17},{2,34}... | collective-permute-start | bytes 1572872 | tf_op jit(solution)/shard_map/ppermute | solution.py:138
  8.0 26.6 %collective-permute-start.3 = (bf16[256,1024]{1,0:T(8,128)(2,1)}, bf16[256,1024]{1,0:T(8,128)(2,1)}, u32[]{:S(2)}, u32[]{:S(2)}) collective-permute-start(bf16[256,1024]{1,0:T(8,128)(2,1)} %join.1.refs_3_.refs_1_), channel_id=1, source_target_pairs={{0,16},{16,32},{32,48},{48,0},{1,17},{17,33},{33,49},{49,1},{2,18}... | collective-permute-start | bytes 1572872 | tf_op jit(solution)/shard_map/ppermute | solution.py:138
  21.3 23.2 %all-to-all-start = ((bf16[8,144,384]{2,1,0:T(8,128)(2,1)}), bf16[8,144,384]{2,1,0:T(8,128)(2,1)}, u32[]{:S(2)}, u32[]{:S(2)}) async-start(bf16[8,144,384]{2,1,0:T(8,128)(2,1)} %pack_q.1.refs_4_), calls=%async_computation | async-start | bytes 1769472 | tf_op jit(solution)/shard_map/all_to_all | solution.py:916
  39.9 26.7 %collective-permute-start.9 = (bf16[2,128,1024]{2,1,0:T(8,128)(2,1)}, bf16[2,128,1024]{2,1,0:T(8,128)(2,1)}, u32[]{:S(2)}, u32[]{:S(2)}) collective-permute-start(bf16[2,128,1024]{2,1,0:T(8,128)(2,1)} %pair.1.refs_3_.refs_6_), channel_id=1, source_target_pairs={{0,6},{2,0},{4,2},{6,4},{1,7},{3,1},{5,3},{7,5},{8,14},{10,8},{12,... | collective-permute-start | bytes 1572872 | tf_op jit(solution)/shard_map/ppermute | solution.py:138
  43.7 33.3 %collective-permute-start.10 = (bf16[2,128,1024]{2,1,0:T(8,128)(2,1)}, bf16[2,128,1024]{2,1,0:T(8,128)(2,1)}, u32[]{:S(2)}, u32[]{:S(2)}) collective-permute-start(bf16[2,128,1024]{2,1,0:T(8,128)(2,1)} %pair.1.refs_3_.refs_6_), channel_id=1, source_target_pairs={{0,4},{2,6},{4,0},{6,2},{1,5},{3,7},{5,1},{7,3},{8,12},{10,14},{12... | collective-permute-start | bytes 1572872 | tf_op jit(solution)/shard_map/ppermute | solution.py:138
  43.7 33.3 %collective-permute-start.11 = (bf16[2,128,1024]{2,1,0:T(8,128)(2,1)}, bf16[2,128,1024]{2,1,0:T(8,128)(2,1)}, u32[]{:S(2)}, u32[]{:S(2)}) collective-permute-start(bf16[2,128,1024]{2,1,0:T(8,128)(2,1)} %pair.1.refs_3_.refs_6_), channel_id=1, source_target_pairs={{0,2},{2,4},{4,6},{6,0},{1,3},{3,5},{5,7},{7,1},{8,10},{10,12},{12... | collective-permute-start | bytes 1572872 | tf_op jit(solution)/shard_map/ppermute | solution.py:138
  51.8 36.5 %collective-permute-start.8 = (bf16[1024,256]{1,0:T(8,128)(2,1)}, bf16[1024,256]{1,0:T(8,128)(2,1)S(1)}, u32[]{:S(2)}, u32[]{:S(2)}) collective-permute-start(bf16[1024,256]{1,0:T(8,128)(2,1)} %get-tuple-element.110.refs_2_), channel_id=1, source_target_pairs={{0,64},{1,65},{2,66},{3,67},{4,68},{5,69},{6,70},{7,71},{8,72},{9,... | collective-permute-start | bytes 1572872 | tf_op jit(solution)/shard_map/ppermute | solution.py:925
  59.4 25.5 %collective-permute-start.24 = (bf16[128,1408]{1,0:T(8,128)(2,1)}, bf16[128,1408]{1,0:T(8,128)(2,1)}, u32[]{:S(2)}, u32[]{:S(2)}) collective-permute-start(bf16[128,1408]{1,0:T(8,128)(2,1)} %pack_second.1.refs_1_), channel_id=1, source_target_pairs={{0,1},{1,0},{2,3},{3,2},{4,5},{5,4},{6,7},{7,6},{8,9},{9,8},{10,11... | collective-permute-start | bytes 1081352 | tf_op jit(solution)/shard_map/ppermute | solution.py:138
  66.5 21.7 %collective-permute-start.12 = (bf16[128,1024]{1,0:T(8,128)(2,1)}, bf16[128,1024]{1,0:T(8,128)(2,1)S(1)}, u32[]{:S(2)}, u32[]{:S(2)}) collective-permute-start(bf16[128,1024]{1,0:T(8,128)(2,1)} %pass_wo.2), channel_id=1, source_target_pairs={{0,0},{1,8},{2,16},{3,24},{4,32},{5,40},{6,48},{7,56},{8,1},{9,9},... | collective-permute-start | bytes 786440 | tf_op jit(solution)/shard_map/ppermute | solution.py:159
  93.5 48.1 %all-to-all-start.1 = ((bf16[4,2,128,1408]{3,2,1,0:T(8,128)(2,1)}), bf16[4,2,128,1408]{3,2,1,0:T(8,128)(2,1)}, u32[]{:S(2)}, u32[]{:S(2)}) async-start(bf16[4,2,128,1408]{3,2,1,0:T(8,128)(2,1)} %gate.3), calls=%async_computation.1 | async-start | bytes 5767168 | tf_op jit(solution)/shard_map/all_to_all | solution.py:961
  147.8 28.7 %collective-permute-start.25 = (bf16[1024,256]{1,0:T(8,128)(2,1)}, bf16[1024,256]{1,0:T(8,128)(2,1)S(1)}, u32[]{:S(2)}, u32[]{:S(2)}) collective-permute-start(bf16[1024,256]{1,0:T(8,128)(2,1)} %get-tuple-element.129.refs_2_), channel_id=1, source_target_pairs={{0,64},{1,65},{2,66},{3,67},{4,68},{5,69},{6,70},{7,71},{8,72},{9,... | collective-permute-start | bytes 1572872 | tf_op jit(solution)/shard_map/ppermute | solution.py:925
  187.7 28.3 %collective-permute-start.31 = (bf16[1024,256]{1,0:T(8,128)(2,1)S(1)}, bf16[1024,256]{1,0:T(8,128)(2,1)S(1)}, u32[]{:S(2)}, u32[]{:S(2)}) collective-permute-start(bf16[1024,256]{1,0:T(8,128)(2,1)S(1)} %get-tuple-element.149), channel_id=1, source_target_pairs={{64,0},{65,1},{66,2},{67,3},{68,4},{69,5},{70,6},{71,7},{72,8},{73... | collective-permute-start | bytes 1572872 | tf_op jit(solution)/shard_map/ppermute | solution.py:987
  190.0 24.6 %collective-permute-start.28 = (bf16[128,1024]{1,0:T(8,128)(2,1)S(1)}, bf16[128,1024]{1,0:T(8,128)(2,1)S(1)}, u32[]{:S(2)}, u32[]{:S(2)}) collective-permute-start(bf16[128,1024]{1,0:T(8,128)(2,1)S(1)} %get-tuple-element.138), channel_id=1, source_target_pairs={{0,16},{16,32},{32,48},{48,0},{1,17},{17,33},{33,49},{49,1},{2,18}... | collective-permute-start | bytes 786440 | tf_op jit(solution)/shard_map/ppermute | solution.py:138
  193.1 21.5 %collective-permute-start.29 = (bf16[128,1024]{1,0:T(8,128)(2,1)S(1)}, bf16[128,1024]{1,0:T(8,128)(2,1)S(1)}, u32[]{:S(2)}, u32[]{:S(2)}) collective-permute-start(bf16[128,1024]{1,0:T(8,128)(2,1)S(1)} %get-tuple-element.139), channel_id=1, source_target_pairs={{0,32},{16,48},{32,0},{48,16},{1,33},{17,49},{33,1},{49,17},{2,34}... | collective-permute-start | bytes 786440 | tf_op jit(solution)/shard_map/ppermute | solution.py:138
  224.9 60.9 %all-to-all-start.2 = ((bf16[8,384,512]{2,1,0:T(8,128)(2,1)}), bf16[8,384,512]{2,1,0:T(8,128)(2,1)}, u32[]{:S(2)}, u32[]{:S(2)}) async-start(bf16[8,384,512]{2,1,0:T(8,128)(2,1)} %get-tuple-element.178), calls=%async_computation.2 | async-start | bytes 6291456 | tf_op jit(solution)/shard_map/all_to_all | solution.py:1003
  276.6 40.8 %collective-permute-start.43 = (bf16[1024,256]{1,0:T(8,128)(2,1)}, bf16[1024,256]{1,0:T(8,128)(2,1)}, u32[]{:S(2)}, u32[]{:S(2)}) collective-permute-start(bf16[1024,256]{1,0:T(8,128)(2,1)} %get-tuple-element.168), channel_id=1, source_target_pairs={{64,0},{65,1},{66,2},{67,3},{68,4},{69,5},{70,6},{71,7},{72,8},{73... | collective-permute-start | bytes 1572872 | tf_op jit(solution)/shard_map/ppermute | solution.py:987
  288.9 27.4 %collective-permute-start.44 = (bf16[352,512]{1,0:T(8,128)(2,1)S(1)}, bf16[352,512]{1,0:T(8,128)(2,1)S(1)}, u32[]{:S(2)}, u32[]{:S(2)}) collective-permute-start(bf16[352,512]{1,0:T(8,128)(2,1)S(1)} %get-tuple-element.179.refs_1_), channel_id=1, source_target_pairs={{0,64},{64,0},{1,65},{65,1},{2,66},{66,2},{3,67},{67,3},{4,68},{68... | collective-permute-start | bytes 1081352 | tf_op jit(solution)/shard_map/ppermute | solution.py:138
  325.4 44.4 %all-to-all-start.3 = ((bf16[8,400,512]{2,1,0:T(8,128)(2,1)}), bf16[8,400,512]{2,1,0:T(8,128)(2,1)}, u32[]{:S(2)}, u32[]{:S(2)}) async-start(bf16[8,400,512]{2,1,0:T(8,128)(2,1)} %get-tuple-element.187), calls=%async_computation.3 | async-start | bytes 6553600 | tf_op jit(solution)/shard_map/all_to_all | solution.py:1026
  330.1 21.8 %collective-permute-start.45 = (bf16[4,128,1024]{2,1,0:T(8,128)(2,1)}, bf16[4,128,1024]{2,1,0:T(8,128)(2,1)S(1)}, u32[]{:S(2)}, u32[]{:S(2)}) collective-permute-start(bf16[4,128,1024]{2,1,0:T(8,128)(2,1)} %get-tuple-element.181), channel_id=1, source_target_pairs={{0,8},{8,0},{1,9},{9,1},{2,10},{10,2},{3,11},{11,3},{4,12},{12,4},... | collective-permute-start | bytes 3145736 | tf_op jit(solution)/shard_map/ppermute | solution.py:138
  332.6 20.3 %collective-permute-start.49 = (bf16[352,512]{1,0:T(8,128)(2,1)S(1)}, bf16[352,512]{1,0:T(8,128)(2,1)S(1)}, u32[]{:S(2)}, u32[]{:S(2)}) collective-permute-start(bf16[352,512]{1,0:T(8,128)(2,1)S(1)} %xsum_top.1.refs_15_.refs_1_), channel_id=1, source_target_pairs={{0,8},{8,0},{1,9},{9,1},{2,10},{10,2},{3,11},{11,3},{4,12},{12,4},... | collective-permute-start | bytes 1081352 | tf_op jit(solution)/shard_map/ppermute | solution.py:138
  395.3 23.5 %collective-permute-start.62 = (bf16[432,512]{1,0:T(8,128)(2,1)S(1)}, bf16[432,512]{1,0:T(8,128)(2,1)S(1)}, u32[]{:S(2)}, u32[]{:S(2)}) collective-permute-start(bf16[432,512]{1,0:T(8,128)(2,1)S(1)} %xsum_last.1.refs_1_), channel_id=1, source_target_pairs={{0,48},{16,0},{32,16},{48,32},{1,49},{17,1},{33,17},{49,33},{2,50}... | collective-permute-start | bytes 1327112 | tf_op jit(solution)/shard_map/ppermute | solution.py:138
  401.6 21.9 %collective-permute-start.66 = (bf16[432,512]{1,0:T(8,128)(2,1)S(1)}, bf16[432,512]{1,0:T(8,128)(2,1)S(1)}, u32[]{:S(2)}, u32[]{:S(2)}) collective-permute-start(bf16[432,512]{1,0:T(8,128)(2,1)S(1)} %xsum_last.1.refs_1_), channel_id=1, source_target_pairs={{0,16},{16,32},{32,48},{48,0},{1,17},{17,33},{33,49},{49,1},{2,18}... | collective-permute-start | bytes 1327112 | tf_op jit(solution)/shard_map/ppermute | solution.py:138
  402.3 21.6 %collective-permute-start.61 = (bf16[432,512]{1,0:T(8,128)(2,1)S(1)}, bf16[432,512]{1,0:T(8,128)(2,1)S(1)}, u32[]{:S(2)}, u32[]{:S(2)}) collective-permute-start(bf16[432,512]{1,0:T(8,128)(2,1)S(1)} %xsum_last.1.refs_1_), channel_id=1, source_target_pairs={{0,8},{8,0},{1,9},{9,1},{2,10},{10,2},{3,11},{11,3},{4,12},{12,4},... | collective-permute-start | bytes 1327112 | tf_op jit(solution)/shard_map/ppermute | solution.py:138
  (103 other events, 1172.9 us)
